TPU v7x, 128 devices: a whole 4x4x4 slice. The times are simulated.
128 devices in a mesh: seq: 8 (over z, core), exp: 16 (over y, x).
Axes of the slice: x: 4, y: 4, z: 4, core: 2. Of those that a mesh axis runs over, the one named last changes fastest.
Arguments:
- tokens: bfloat16 [16384, 2048], P(('seq', 'exp')), may hold values from -6 to 6
- norm_in: float32 [2048], replicated, may hold values from 0.1 to 1.9
- w_query: bfloat16 [2048, 2048], P(None, 'exp'), may hold values from -0.125 to 0.125
- w_key: bfloat16 [2048, 2048], P(None, 'exp'), may hold values from -0.125 to 0.125
- w_value: bfloat16 [2048, 4096], P(None, 'exp'), may hold values from -0.125 to 0.125
- w_outgate: bfloat16 [2048, 4096], P(None, 'exp'), may hold values from -0.125 to 0.125
- log_decay: float32 [32, 16384], P('exp', 'seq'), may hold values from -1 to 0, as said below
- write_rate: float32 [32, 16384], P('exp', 'seq'), may hold values from 0.005 to 0.95
- head_gain: float32 [128], replicated, may hold values from 0.1 to 1.9
- w_output: bfloat16 [4096, 2048], P('exp'), may hold values from -0.09375 to 0.09375
- norm_post: float32 [2048], replicated, may hold values from 0.1 to 1.9
- route_ids: int32 [16384, 10], P('seq'), may hold values from 0 to 31, all different within a row; in each aligned block of 128 rows (0 to 127, 128 to 255, ...) at most 80 rows name the same one
- route_weights: float32 [16384, 10], P('seq'), may hold values from 0.1 to 0.5
- w_gate: bfloat16 [32, 2048, 512], P('exp'), may hold values from -0.125 to 0.125
- w_up: bfloat16 [32, 2048, 512], P('exp'), may hold values from -0.125 to 0.125
- w_down: bfloat16 [32, 512, 2048], P('exp'), may hold values from -0.25 to 0.25
- w_shared_gate: bfloat16 [2048, 512], replicated, may hold values from -0.125 to 0.125
- w_shared_up: bfloat16 [2048, 512], replicated, may hold values from -0.125 to 0.125
- w_shared_down: bfloat16 [512, 2048], replicated, may hold values from -0.25 to 0.25
- w_shared_switch: bfloat16 [2048], replicated, may hold values from -0.125 to 0.125
Outputs:
- layer_out: bfloat16 [16384, 2048], P(('seq', 'exp'))
Inputs may be any that keep to these rules, and one draw needn't show every extreme that they name: `route_ids`: each row names 10 different experts. In each aligned block of 128 rows (the tokens of one device) no expert is named by more than 80 rows. `log_decay`: never positive.
All inputs are finite; a program needn't handle non-finite values.
Results may differ from a plain program's by a relative error of at most 0.023.
Values may be sent and summed in bfloat16 or wider, within the bound.
No kernel may reach another device: no remote copies, remote signals or barrier semaphores. Data moves between devices by JAX's collectives and lax.ppermute only.
A program may use at most 192 MiB of HBM per device.

v0:
```python
import jax
import jax.numpy as jnp
from jax import lax
from jax.experimental import pallas as pl
from jax.experimental.pallas import tpu as pltpu
from jax.sharding import PartitionSpec as P

DK = 128
DV = 128
BLOCK = 128
F32 = jnp.float32
BF16 = jnp.bfloat16
NN = (((1,), (0,)), ((), ()))
NT = (((1,), (1,)), ((), ()))
TN = (((0,), (0,)), ((), ()))


def row_norm(values, gain_vec, epsilon):
    return (
        values * lax.rsqrt(jnp.mean(values * values, axis=-1, keepdims=True) + epsilon) * gain_vec
    )


def split(x):
    hi = x.astype(BF16)
    return hi, (x - hi.astype(F32)).astype(BF16)


def mm(a, b, dims=NN):
    return lax.dot_general(a, b, dims, preferred_element_type=F32)


def dot3_narrow(a, b):
    ah, al = split(a)
    bh, bl = split(b)
    left = jnp.concatenate([ah, al], axis=1)
    right = jnp.concatenate(
        [jnp.concatenate([bh, bl], axis=1), jnp.concatenate([bh, jnp.zeros_like(bl)], axis=1)],
        axis=0,
    )
    both = mm(left, right)
    return both[:, :128] + both[:, 128:]


def dot3_wide(a, b):
    ah, al = split(a)
    bh, bl = split(b)
    return mm(jnp.concatenate([ah, al], axis=1), jnp.concatenate([bh, bh], axis=0)) + mm(ah, bl)


def delta_kernel(
    blocks,
    place_ref,
    *refs,
):
    gathered, refs = refs[: 2 * SIDE], refs[2 * SIDE :]
    query_ref, key_ref, value_ref, outgate_ref, cum_ref, rate_ref = refs[:6]
    base_ref, reach_ref, gate_ref, total_ref, state, held, lines, proj_ref, arrived = refs[6:]
    step = pl.program_id(0)

    @pl.when(step == 0)
    def _():
        copies = [
            pltpu.make_async_copy(ref, held.at[i // SIDE, i % SIDE], arrived.at[i])
            for i, ref in enumerate(gathered)
        ]
        for copy in copies:
            copy.start()
        for copy in copies:
            copy.wait()

    part = held.shape[3]
    pair = 2

    def project(c, carry):
        for u in range(pair):
            block = c * pair + u
            far_y = lax.rem(step * (blocks // SIDE) + block // SIDE - place_ref[0] + SIDE, SIDE)
            far_x = lax.rem(block % SIDE - place_ref[1] + SIDE, SIDE)
            lines[u * BLOCK : u * BLOCK + part] = held[0, far_y, far_x]
            lines[u * BLOCK + part : (u + 1) * BLOCK] = held[1, far_x, far_y]
        x = lines[...]
        span = pl.ds(pl.multiple_of(c * pair * BLOCK, pair * BLOCK), pair * BLOCK)
        proj_ref[span, 0:DK] = mm(x, query_ref[...])
        proj_ref[span, DK : 2 * DK] = mm(x, key_ref[...])
        proj_ref[span, 2 * DK :] = mm(x, value_ref[...])
        gate_ref[span, :] = mm(x, outgate_ref[...])
        return carry

    lax.fori_loop(0, blocks // pair, project, 0)
    rows = lax.broadcasted_iota(jnp.int32, (BLOCK, BLOCK), 0)
    cols = lax.broadcasted_iota(jnp.int32, (BLOCK, BLOCK), 1)
    causal = rows >= cols
    strict = rows > cols
    apart = rows ^ cols
    eye = jnp.where(rows == cols, 1.0, 0.0).astype(F32)
    heads = 2

    @pl.when(step == 0)
    def _():
        for h in range(heads):
            state[h] = jnp.concatenate([eye, jnp.zeros((DK, DV), F32)], axis=1)

    problems = []
    for b in range(blocks):
        span = slice(b * BLOCK, (b + 1) * BLOCK)
        query = proj_ref[span, 0:DK]
        key = proj_ref[span, DK : 2 * DK]
        key = key * lax.rsqrt(jnp.sum(key * key, axis=-1, keepdims=True) + 1e-06)
        qh, ql = split(query)
        kh, kl = split(key)
        stacked_h = jnp.concatenate([kh, qh], axis=0)
        stacked_l = jnp.concatenate([kl, ql], axis=0)
        products = mm(stacked_h, kh, NT) + (mm(stacked_h, kl, NT) + mm(stacked_l, kh, NT))
        key_key, query_key = products[:BLOCK], products[BLOCK:]
        for h in range(heads):
            cum_row = jnp.broadcast_to(cum_ref[h, b : b + 1, :], (BLOCK, BLOCK))
            rate_row = jnp.broadcast_to(rate_ref[h, b : b + 1, :], (BLOCK, BLOCK))
            cum_col = cum_row.T
            rate_col = rate_row.T
            ratios = jnp.where(causal, jnp.exp(jnp.where(causal, cum_col - cum_row, 0.0)), 0.0)
            weighted = ratios * rate_row
            lower = jnp.where(strict, weighted * key_key, 0.0)
            mixing = weighted * query_key
            decays = jnp.exp(cum_col)
            last = cum_col[BLOCK - 1 : BLOCK, :]
            key_tail = key * (jnp.exp(last - cum_col) * rate_col)
            value = proj_ref[span, 2 * DK + h * DV : 2 * DK + (h + 1) * DV]
            problems.append(
                dict(
                    b=b,
                    h=h,
                    lower=lower,
                    mixing=mixing,
                    right=jnp.concatenate([value, decays * key], axis=1),
                    query=decays * query,
                    key_tail=key_tail,
                    fade=jnp.exp(last) * eye,
                    inverse=eye - jnp.where(apart == 1, lower, 0.0),
                )
            )
    size = 2
    while size < BLOCK:
        for p in problems:
            part = jnp.where((apart >= size) & (apart < 2 * size), p["lower"], 0.0)
            p["inner"] = dot3_narrow(part, p["inverse"])
        for p in problems:
            p["inverse"] = p["inverse"] - dot3_narrow(p["inverse"], p["inner"])
        size *= 2
    for p in problems:
        p["solved"] = dot3_wide(p["inverse"], p["right"])
    for p in problems:
        p["mixed"] = dot3_wide(p["mixing"], p["solved"])
        p["tail"] = dot3_wide(p["key_tail"].T, p["solved"])
    for p in problems:
        h = p["h"]
        span = slice(p["b"] * BLOCK, (p["b"] + 1) * BLOCK)
        cols_h = slice(h * DV, (h + 1) * DV)
        before = state[h]
        effective = p["query"] - p["mixed"][:, DV:]
        seen = dot3_wide(effective, before)
        reach_ref[span, cols_h] = seen[:, :DK]
        base_ref[span, cols_h] = p["mixed"][:, :DV] + seen[:, DK:]
        moved = dot3_wide(p["fade"] - p["tail"][:, DV:], before)
        state[h] = jnp.concatenate([moved[:, :DK], moved[:, DK:] + p["tail"][:, :DV]], axis=1)

    @pl.when(step == pl.num_programs(0) - 1)
    def _():
        total_ref[...] = state[...]


def delta_local(place, firsts, seconds, weights, cumulative, rates):
    side, part, width = firsts[0].shape
    tokens = 2 * side * side * part
    blocks = 8
    whole = lambda i, p: (0, 0)
    lines = pl.BlockSpec((blocks * BLOCK, 2 * DV), lambda i, p: (i, 0))
    rates_spec = pl.BlockSpec((2, blocks, BLOCK), lambda i, p: (0, i, 0))
    return pl.pallas_call(
        lambda *refs: delta_kernel(blocks, *refs),
        grid_spec=pltpu.PrefetchScalarGridSpec(
            num_scalar_prefetch=1,
            grid=(tokens // (blocks * BLOCK),),
            in_specs=[pl.BlockSpec(memory_space=pl.ANY)] * (2 * side)
            + [pl.BlockSpec(w.shape, whole, pipeline_mode=pl.Buffered(1)) for w in weights]
            + [rates_spec, rates_spec],
            out_specs=[
                lines,
                lines,
                lines,
                pl.BlockSpec((2, DK, DK + DV), lambda i, p: (0, 0, 0)),
            ],
            scratch_shapes=[
                pltpu.VMEM((2, DK, DK + DV), F32),
                pltpu.VMEM((2, side, side, part, width), BF16),
                pltpu.VMEM((2 * BLOCK, width), BF16),
                pltpu.VMEM((blocks * BLOCK, 2 * DK + 2 * DV), F32),
                pltpu.SemaphoreType.DMA((2 * side,)),
            ],
        ),
        out_shape=[jax.ShapeDtypeStruct((tokens, 2 * DV), F32)] * 3
        + [jax.ShapeDtypeStruct((2, DK, DK + DV), F32)],
        compiler_params=pltpu.CompilerParams(vmem_limit_bytes=60 * 2**20),
        cost_estimate=pl.CostEstimate(
            flops=3 * 10**10, bytes_accessed=2 * 10**7, transcendentals=0
        ),
        name="delta_local",
    )(place, *firsts, *seconds, *weights, cumulative, rates)


def gate_kernel(
    place_ref, maps_ref, base_ref, reach_ref, gate_ref, gain_ref, out_ref, entering
):
    @pl.when(pl.program_id(0) == 0)
    def _():
        states = [jnp.zeros((DK, DV), F32)] * 2
        for j in range(maps_ref.shape[0]):
            for h in range(2):
                pair = maps_ref[j, h]
                high, low = split(states[h])
                moved = mm(pair[:, :DK], jnp.concatenate([high, low], axis=1))
                states[h] = moved[:, :DV] + moved[:, DV:] + pair[:, DK:].astype(F32)
                if j == maps_ref.shape[0] - 2:
                    entering[h] = states[h]
        for h in range(2):
            entering[h] = jnp.where(place_ref[2] == 1, states[h], entering[h])

    for h in range(2):
        span = slice(h * DV, (h + 1) * DV)
        attended = base_ref[:, span] + dot3_narrow(reach_ref[:, span], entering[h])
        scaled = row_norm(attended, gain_ref[...], 1e-06)
        u = gate_ref[:, span]
        out_ref[:, span] = (scaled * (u / (1.0 + jnp.exp(-u)))).astype(out_ref.dtype)


def delta_gate(place, maps, base, reach, gate, gain):
    tokens = base.shape[0]
    rows = 512
    lines = pl.BlockSpec((rows, 2 * DV), lambda i, p: (i, 0))
    return pl.pallas_call(
        gate_kernel,
        grid_spec=pltpu.PrefetchScalarGridSpec(
            num_scalar_prefetch=1,
            grid=(tokens // rows,),
            in_specs=[
                pl.BlockSpec(maps.shape, lambda i, p: (0, 0, 0, 0)),
                lines,
                lines,
                lines,
                pl.BlockSpec((1, DV), lambda i, p: (0, 0)),
            ],
            out_specs=lines,
            scratch_shapes=[pltpu.VMEM((2, DK, DV), F32)],
        ),
        out_shape=jax.ShapeDtypeStruct((tokens, 2 * DV), BF16),
        compiler_params=pltpu.CompilerParams(vmem_limit_bytes=60 * 2**20),
        cost_estimate=pl.CostEstimate(flops=10**9, bytes_accessed=10**7, transcendentals=10**6),
        name="delta_gate",
    )(place, maps, base, reach, gate, gain)


def expert_kernel(xa_ref, xb_ref, sa_ref, sb_ref, gate_ref, up_ref, down_ref, oa_ref, ob_ref, x_ref, total):
    width = xa_ref.shape[-1]
    rows = xa_ref.size // width
    step = pl.program_id(0)
    expert = step // EXPERT_CUTS

    @pl.when(step == 0)
    def _():
        x_ref[:rows] = xa_ref[...].reshape(rows, width)
        x_ref[rows:] = xb_ref[...].reshape(rows, width)

    x = x_ref[...]
    shares = jnp.concatenate(
        [sa_ref[...].reshape(rows, -1), sb_ref[...].reshape(rows, -1)], axis=0
    )
    share = jnp.where(expert == 0, shares[:, 0:1], shares[:, 1:2])
    gated = mm(x, gate_ref[0])
    raised = mm(x, up_ref[0])
    hidden = gated / (1.0 + jnp.exp(-gated)) * raised * share
    made = mm(hidden.astype(BF16), down_ref[0])

    @pl.when(step == 0)
    def _():
        total[...] = made

    @pl.when((step > 0) & (step < pl.num_programs(0) - 1))
    def _():
        total[...] += made

    @pl.when(step == pl.num_programs(0) - 1)
    def _():
        done = (total[...] + made).astype(oa_ref.dtype)
        oa_ref[...] = done[:rows].reshape(oa_ref.shape)
        ob_ref[...] = done[rows:].reshape(ob_ref.shape)


EXPERT_CUTS = 2


def expert_mix(xa, xb, sa, sb, w_gate, w_up, w_down):
    side, part, width = xa.shape
    count, _, inner = w_gate.shape
    cut = inner // EXPERT_CUTS
    whole = lambda i: (0, 0, 0)
    rows_spec = pl.BlockSpec((side, part, width), whole, pipeline_mode=pl.Buffered(1))
    share_spec = pl.BlockSpec((side, part, count), whole, pipeline_mode=pl.Buffered(1))
    out_spec = pl.BlockSpec((side, part, width), whole)
    across = pl.BlockSpec((1, width, cut), lambda i: (i // EXPERT_CUTS, 0, i % EXPERT_CUTS))
    down = pl.BlockSpec((1, cut, width), lambda i: (i // EXPERT_CUTS, i % EXPERT_CUTS, 0))
    return pl.pallas_call(
        expert_kernel,
        grid=(count * EXPERT_CUTS,),
        in_specs=[rows_spec, rows_spec, share_spec, share_spec, across, across, down],
        out_specs=[out_spec, out_spec],
        out_shape=[jax.ShapeDtypeStruct((side, part, width), BF16)] * 2,
        scratch_shapes=[
            pltpu.VMEM((2 * side * part, width), BF16),
            pltpu.VMEM((2 * side * part, width), F32),
        ],
        compiler_params=pltpu.CompilerParams(vmem_limit_bytes=48 * 2**20),
        cost_estimate=pl.CostEstimate(
            flops=12 * side * part * count * width * inner,
            bytes_accessed=6 * count * width * inner + 8 * side * part * width,
            transcendentals=2 * side * part * count * inner,
        ),
        name="expert_mix",
    )(xa, xb, sa, sb, w_gate, w_up, w_down)


SIDE = 4


def neighbour(value, axis, by):
    pairs = []
    for y in range(SIDE):
        for x in range(SIDE):
            ny, nx = ((y + by) % SIDE, x) if axis == 0 else (y, (x + by) % SIDE)
            pairs.append((y * SIDE + x, ny * SIDE + nx))
    return lax.ppermute(value, "exp", pairs)


def plus(*terms):
    total = terms[0].astype(F32)
    for term in terms[1:]:
        total = total + term.astype(F32)
    return total


def far_sums(groups, axis):
    far = groups(2)
    half = far.shape[0] // 2
    return neighbour(far[:half], axis, 1), neighbour(far[half:], axis, -1)


def near_sums(groups, axis, up, down, final):
    half = up.shape[0]
    ahead, behind = groups(1), groups(-1)
    ahead = jnp.concatenate([plus(ahead[:half], up).astype(BF16), ahead[half:]], axis=0)
    behind = jnp.concatenate([behind[:half], plus(behind[half:], down).astype(BF16)], axis=0)
    from_behind = neighbour(ahead, axis, 1)
    from_ahead = neighbour(behind, axis, -1)
    return plus(groups(0), from_behind, from_ahead).astype(final)


def scatter_sums(first, second):
    up_a, down_a = far_sums(first, 0)
    up_b, down_b = far_sums(second, 1)
    up_a, down_a, up_b, down_b = lax.optimization_barrier((up_a, down_a, up_b, down_b))
    a = near_sums(first, 0, up_a, down_a, BF16)
    b = near_sums(second, 1, up_b, down_b, BF16)
    first, second = (lambda k: a[k % SIDE]), (lambda k: b[k % SIDE])
    a_last = near_sums(first, 1, *far_sums(first, 1), F32)
    b_last = near_sums(second, 0, *far_sums(second, 0), F32)
    return jnp.concatenate([a_last, b_last], axis=0)


def gather_direct(block, axis):
    return [
        block,
        neighbour(block, axis, -1),
        neighbour(block, axis, 2),
        neighbour(block, axis, 1),
    ]


def gather_rows(rows, beside=None):
    tie = (lambda v: v) if beside is None else lax.optimization_barrier
    part = rows.shape[0] // 2
    a, b = gather_direct(rows[:part], 1), gather_direct(rows[part:], 0)
    a, b = tie((a, b))
    a, b = jnp.stack(a), jnp.stack(b)
    half = a.shape[0] // 2
    a_behind, a_ahead = neighbour(a, 0, 1), neighbour(a, 0, -1)
    b_behind, b_ahead = neighbour(b, 1, 1), neighbour(b, 1, -1)
    a_behind, a_ahead, b_behind, b_ahead, beside = tie(
        (a_behind, a_ahead, b_behind, b_ahead, beside)
    )
    a_far = (neighbour(a_behind[:half], 0, 1), neighbour(a_ahead[half:], 0, -1))
    b_far = (neighbour(b_behind[:half], 1, 1), neighbour(b_ahead[half:], 1, -1))
    first = [a, a_ahead, jnp.concatenate(a_far, axis=0), a_behind]
    second = [b, b_ahead, jnp.concatenate(b_far, axis=0), b_behind]
    return first, second, beside


def along_seq(value, pairs):
    return lax.ppermute(value, "seq", pairs)


def other_core(value):
    return along_seq(value, [(i, i ^ 1) for i in range(lax.axis_size("seq"))])


def relay(total, core):
    mine = total.astype(BF16)
    theirs = other_core(mine)
    early = jnp.where(core == 0, mine, theirs)
    late = jnp.where(core == 0, theirs, mine)
    chip = jnp.einsum("hkl,hlm->hkm", late[:, :, :DK], early, preferred_element_type=F32)
    chip = jnp.concatenate([chip[:, :, :DK], chip[:, :, DK:] + late[:, :, DK:].astype(F32)], axis=2)
    chip = chip.astype(BF16)
    size = lax.axis_size("seq")
    shifts = [along_seq(chip, [(i, i + 2 * d) for i in range(size - 2 * d)]) for d in (3, 2, 1)]
    return jnp.stack(shifts + [theirs])


def local(
    tokens,
    norm_in,
    w_query,
    w_key,
    w_value,
    w_outgate,
    log_decay,
    write_rate,
    head_gain,
    w_output,
    norm_post,
    route_ids,
    route_weights,
    w_gate,
    w_up,
    w_down,
    w_shared_gate,
    w_shared_up,
    w_shared_down,
    w_shared_switch,
):
    tok_dev = tokens.shape[0]
    owners = lax.axis_size("exp")
    tok_seq = tok_dev * owners
    position = lax.axis_index("exp")
    residual_in = tokens.astype(F32)
    normed = row_norm(residual_in, norm_in, 1e-06).astype(BF16)
    y, x = position // SIDE, position % SIDE
    core = lax.axis_index("seq") % 2
    place = jnp.stack([y, x, core]).astype(jnp.int32)
    half = w_output.shape[1] // 2
    w_half = lax.dynamic_slice_in_dim(w_output, core * half, half, 1)
    firsts, seconds, w_half = gather_rows(normed, w_half)
    w_half = lax.all_gather(w_half, "exp", axis=0)
    blocks = tok_seq // BLOCK
    cumulative = jnp.cumsum(log_decay.reshape(2, blocks, BLOCK), axis=-1)
    weights = (w_query, w_key, w_value, w_outgate)
    base, reach, gate, total = delta_local(
        place, firsts, seconds, weights, cumulative, write_rate.reshape(2, blocks, BLOCK)
    )
    maps = relay(total, core)
    gated = delta_gate(place, maps, base, reach, gate, head_gain.reshape(1, DV))
    arrived = lax.all_to_all(
        gated.reshape(owners, tok_dev, -1), "exp", split_axis=0, concat_axis=0, tiled=True
    )
    theirs = other_core(arrived)
    mix = lambda rows: jnp.einsum("stc,scd->td", rows, w_half, preferred_element_type=F32)
    back = other_core(mix(theirs).astype(BF16)).astype(F32)
    kept = mix(arrived)
    mixed_out = jnp.concatenate(
        [jnp.where(core == 0, kept, back), jnp.where(core == 0, back, kept)], axis=1
    )
    residual = residual_in + mixed_out
    post_norm = row_norm(residual, norm_post, 1e-06).astype(BF16)
    rows_first, rows_second, _ = gather_rows(post_norm)
    switch = jax.nn.sigmoid(jnp.dot(post_norm, w_shared_switch, preferred_element_type=F32))
    inner_act = (
        jax.nn.silu(jnp.dot(post_norm, w_shared_gate, preferred_element_type=F32))
        * jnp.dot(post_norm, w_shared_up, preferred_element_type=F32)
    ).astype(BF16)
    shared = jnp.dot(inner_act, w_shared_down, preferred_element_type=F32) * switch[:, None]
    count = w_gate.shape[0]
    mine = position * count + jnp.arange(count, dtype=jnp.int32)
    shares = jnp.sum(
        jnp.where(route_ids[:, :, None] == mine, route_weights[:, :, None], 0.0), axis=1
    )
    shares = jnp.roll(shares.T.reshape(count, SIDE, SIDE, 2, tok_dev // 2), (-y, -x), (1, 2))
    share_first = jnp.transpose(shares[:, :, :, 0], (1, 2, 3, 0))
    share_second = jnp.transpose(shares[:, :, :, 1], (2, 1, 3, 0))
    made = {}
    previous = None
    for k in (0, 1, 2, 3):
        xa, xb = rows_first[k], rows_second[k]
        if previous is None:
            xa, xb, shared = lax.optimization_barrier((xa, xb, shared))
        else:
            xa, xb, *made[previous] = lax.optimization_barrier((xa, xb, *made[previous]))
        made[k] = expert_mix(xa, xb, share_first[k], share_second[k], w_gate, w_up, w_down)
        previous = k
    routed = scatter_sums(lambda k: made[k % SIDE][0], lambda k: made[k % SIDE][1])
    return (residual + shared + routed).astype(BF16)


def solution(mesh):
    in_specs = (
        P(("seq", "exp"), None),
        P(),
        P(None, "exp"),
        P(None, "exp"),
        P(None, "exp"),
        P(None, "exp"),
        P("exp", "seq"),
        P("exp", "seq"),
        P(),
        P("exp", None),
        P(),
        P("seq", None),
        P("seq", None),
        P("exp", None, None),
        P("exp", None, None),
        P("exp", None, None),
        P(),
        P(),
        P(),
        P(),
    )
    out_specs = P(("seq", "exp"), None)
    return jax.shard_map(local, mesh=mesh, in_specs=in_specs, out_specs=out_specs, check_vma=False)
```

profile of v0, /device:TPU:32, one launch (start us, length us, event | category | flops | bytes accessed | tf_op | source)
XLA Modules:
  0.0 343.0 jit_solution(7959264085922491092)
XLA Ops:
  9.2 2.8 collective-permute-start
  13.7 3.0 collective-permute-start.3
  17.4 5.9 %collective-permute-done = bf16[64,2048]{1,0:T(8,128)(2,1)S(1)} collective-permute-done((bf16[64,2048]{1,0:T(8,128)(2,1)S(1)}, bf16[64,2048]{1,0:T(8,128)(2,1)S(1)}, u32[]{:S(2)}, u32[]{:S(2)}) %collective-permute-start) | collective-permute-done | bytes 262176 | tf_op jit(solution)/shard_map/ppermute | solution.py:340
  24.8 2.1 collective-permute-done.2
  27.5 3.3 collective-permute-done.5
  32.8 2.9 collective-permute-start.9
  37.1 2.9 collective-permute-start.7
  40.0 1.9 constant_dynamic-slice_fusion
  41.9 15.2 %collective-permute-done.8.refs_8_ = bf16[4,64,2048]{2,1,0:T(8,128)(2,1)} collective-permute-done((bf16[4,64,2048]{2,1,0:T(8,128)(2,1)S(1)}, bf16[4,64,2048]{2,1,0:T(8,128)(2,1)}, u32[]{:S(2)}, u32[]{:S(2)}) %collective-permute-start.8) | collective-permute-done | bytes 1048608 | tf_op jit(solution)/shard_map/ppermute | solution.py:340
  57.7 3.5 %collective-permute-done.6.refs_4_ = bf16[4,64,2048]{2,1,0:T(8,128)(2,1)} collective-permute-done((bf16[4,64,2048]{2,1,0:T(8,128)(2,1)}, bf16[4,64,2048]{2,1,0:T(8,128)(2,1)}, u32[]{:S(2)}, u32[]{:S(2)}) %collective-permute-start.6) | collective-permute-done | bytes 1048608 | tf_op jit(solution)/shard_map/ppermute | solution.py:340
  61.2 1.9 slice.207
  64.0 1.9 slice.208
  65.8 2.4 collective-permute-start.13
  70.8 3.4 %collective-permute-start.11 = (bf16[2,64,2048]{2,1,0:T(8,128)(2,1)S(1)}, bf16[2,64,2048]{2,1,0:T(8,128)(2,1)}, u32[]{:S(2)}, u32[]{:S(2)}) collective-permute-start(bf16[2,64,2048]{2,1,0:T(8,128)(2,1)S(1)} %slice.206), channel_id=1, source_target_pairs={{0,12},{1,13},{2,14},{3,15},{4,0},{5,1},{6,2},{7,3},{8,4},{9,5},{1... | collective-permute-start | bytes 1572872 | tf_op jit(solution)/shard_map/ppermute | solution.py:340
  77.0 6.5 %collective-permute-done.13 = bf16[2,64,2048]{2,1,0:T(8,128)(2,1)} collective-permute-done((bf16[2,64,2048]{2,1,0:T(8,128)(2,1)}, bf16[2,64,2048]{2,1,0:T(8,128)(2,1)}, u32[]{:S(2)}, u32[]{:S(2)}) %collective-permute-start.13) | collective-permute-done | bytes 524320 | tf_op jit(solution)/shard_map/ppermute | solution.py:340
  83.5 2.3 pad_maximum_fusion.3.refs_7_
  85.8 3.6 %collective-permute-done.10 = bf16[2,64,2048]{2,1,0:T(8,128)(2,1)} collective-permute-done((bf16[2,64,2048]{2,1,0:T(8,128)(2,1)S(1)}, bf16[2,64,2048]{2,1,0:T(8,128)(2,1)}, u32[]{:S(2)}, u32[]{:S(2)}) %collective-permute-start.10) | collective-permute-done | bytes 524320 | tf_op jit(solution)/shard_map/ppermute | solution.py:340
  90.1 2.3 pad_maximum_fusion.2.refs_3_
  92.4 34.3 %delta_local.1 = (f32[2048,256]{1,0:T(8,128)}, f32[2048,256]{1,0:T(8,128)}, f32[2048,256]{1,0:T(8,128)}, f32[2,128,256]{2,1,0:T(8,128)}) custom-call(s32[3]{0:T(128)} %pad_add_fusion.refs_0_.place_ref, bf16[4,64,2048]{2,1,0:T(8,128)(2,1)} %pad_maximum_fusion.refs_1_, bf16[4,64,2048]{2,1,0:T(8,128)(2,1)} %collective-permute-done.7.refs_2_, ...), custom_call_target="tpu_custom_call" | custom-call | flops 30000001024 | bytes 20000000 | tf_op jit(solution)/shard_map/delta_local/pallas_call | solution.py:179
  131.0 5.9 %collective-permute-start.16 = (bf16[2,128,256]{2,1,0:T(8,128)(2,1)S(1)}, bf16[2,128,256]{2,1,0:T(8,128)(2,1)S(1)}, u32[]{:S(2)}, u32[]{:S(2)}) collective-permute-start(bf16[2,128,256]{2,1,0:T(8,128)(2,1)S(1)} %pad_maximum_fusion.17), channel_id=1, source_target_pairs={{0,64},{16,80},{32,96},{48,112},{1,65},{17,81},{33,97},{49,113},{2... | collective-permute-start | bytes 393224 | tf_op jit(solution)/shard_map/ppermute | solution.py:407
  136.9 1.9 collective-permute-start.17
  140.0 4.4 %collective-permute-done.17 = bf16[2,128,256]{2,1,0:T(8,128)(2,1)S(1)} collective-permute-done((bf16[2,128,256]{2,1,0:T(8,128)(2,1)S(1)}, bf16[2,128,256]{2,1,0:T(8,128)(2,1)S(1)}, u32[]{:S(2)}, u32[]{:S(2)}) %collective-permute-start.17) | collective-permute-done | bytes 131104 | tf_op jit(solution)/shard_map/ppermute | solution.py:407
  145.2 6.8 %delta_gate.1 = bf16[2048,256]{1,0:T(8,128)(2,1)} custom-call(s32[3]{0:T(128)} %pad_add_fusion.refs_0_.place_ref, bf16[4,2,128,256]{3,2,1,0:T(8,128)(2,1)} %pad_maximum_fusion.12.maps_ref, f32[2048,256]{1,0:T(8,128)} %get-tuple-element.62.base_ref, f32[2048,256]{1,0:T(8,128)} %get-tuple-element.63.reach_ref, f32[2048,256]{1,0:T(8,128)} %get-tuple-element.64.gate_ref, ...), custom_call_target="tpu_custom_call" | custom-call | flops 1000000000 | bytes 10000000 | tf_op jit(solution)/shard_map/delta_gate/pallas_call | solution.py:240
  152.0 22.9 %all_to_all.5 = bf16[16,128,256]{2,1,0:T(8,128)(2,1)S(1)} all-to-all(bf16[16,128,256]{2,1,0:T(8,128)(2,1)} %bitcast.136), channel_id=1, replica_groups=mesh['seq'=8,'exp'=16] {'exp'}, dimensions={0} | all-to-all | bytes 2097152 | tf_op jit(solution)/shard_map/all_to_all | solution.py:470
  179.6 5.1 %fusion = bf16[128,1024]{1,0:T(8,128)(2,1)S(1)} fusion(bf16[16,128,256]{2,1,0:T(8,128)(2,1)} %collective-permute-done.18, bf16[16,256,1024]{2,1,0:T(8,128)(2,1)} %bitcast.134), kind=kOutput, calls=%fused_computation.12 | convolution fusion | flops 1073872896 | bytes 9699328 | tf_op jit(solution)/shard_map/stc,scd->td/dot_general | solution.py:474
  195.3 2.6 collective-permute-done.23
  199.6 2.2 collective-permute-done.24
  201.9 4.8 %collective-permute-done.25 = bf16[64,2048]{1,0:T(8,128)(2,1)S(1)} collective-permute-done((bf16[64,2048]{1,0:T(8,128)(2,1)S(1)}, bf16[64,2048]{1,0:T(8,128)(2,1)S(1)}, u32[]{:S(2)}, u32[]{:S(2)}) %collective-permute-start.25) | collective-permute-done | bytes 262176 | tf_op jit(solution)/shard_map/ppermute | solution.py:340
  210.0 2.5 collective-permute-start.26
  212.9 3.6 %convolution_multiply_fusion = f32[128,2048]{1,0:T(8,128)} fusion(bf16[512,2048]{1,0:T(8,128)(2,1)S(1)} %copy-done, bf16[128,2048]{1,0:T(8,128)(2,1)} %copy-done.8, bf16[2048,512]{1,0:T(8,128)(2,1)} %param.37, f32[128]{0:T(128)S(1)} %fusion.5, f32[128,512]{1,0:T(8,128)} %fusion.34), kind=kOutput, calls=%fused_computation | convolution fusion | flops 537526272 | bytes 6029824 | tf_op jit(solution)/shard_map/dot_general | solution.py:488
  218.3 11.5 %expert_mix.4 = (bf16[4,64,2048]{2,1,0:T(8,128)(2,1)S(1)}, bf16[4,64,2048]{2,1,0:T(8,128)(2,1)S(1)}) custom-call(bf16[4,64,2048]{2,1,0:T(8,128)(2,1)} %pad_maximum_fusion.4.xa_ref, bf16[4,64,2048]{2,1,0:T(8,128)(2,1)S(1)} %pad_maximum_fusion.5.xb_ref, f32[4,64,2]{2,1,0:T(8,128)S(1)} %copy-done.6, f32[4,64,2]{2,1,0:T(8,128)S(1)} %copy-done.5, ...), custom_call_target="tpu_custom_call" | custom-call | flops 6442450944 | bytes 16777216 | tf_op jit(solution)/shard_map/expert_mix/pallas_call | solution.py:311
  229.9 2.2 collective-permute-done.27.xb_ref
  232.1 3.3 collective-permute-done.26.xa_ref
  237.8 3.1 collective-permute-start.33
  244.5 2.4 collective-permute-start.30
  247.0 11.9 %expert_mix.5 = (bf16[4,64,2048]{2,1,0:T(8,128)(2,1)S(1)}, bf16[4,64,2048]{2,1,0:T(8,128)(2,1)S(1)}) custom-call(bf16[4,64,2048]{2,1,0:T(8,128)(2,1)} %collective-permute-done.26.xa_ref, bf16[4,64,2048]{2,1,0:T(8,128)(2,1)} %collective-permute-done.27.xb_ref, f32[4,64,2]{2,1,0:T(8,128)S(1)} %copy-done.4, f32[4,64,2]{2,1,0:T(8,128)S(1)} %copy-done.3, ...), custom_call_target="tpu_custom_call" | custom-call | flops 6442450944 | bytes 16777216 | tf_op jit(solution)/shard_map/expert_mix/pallas_call | solution.py:311
  259.7 10.9 %expert_mix.6 = (bf16[4,64,2048]{2,1,0:T(8,128)(2,1)S(1)}, bf16[4,64,2048]{2,1,0:T(8,128)(2,1)S(1)}) custom-call(bf16[4,64,2048]{2,1,0:T(8,128)(2,1)S(1)} %pad_maximum_fusion.6.xa_ref, bf16[4,64,2048]{2,1,0:T(8,128)(2,1)S(1)} %pad_maximum_fusion.7.xb_ref, f32[4,64,2]{2,1,0:T(8,128)S(1)} %copy-done.2, f32[4,64,2]{2,1,0:T(8,128)S(1)} %get-tuple-element.114.sb_ref, ...), custom_call_target="tpu_custom_call" | custom-call | flops 6442450944 | bytes 16777216 | tf_op jit(solution)/shard_map/expert_mix/pallas_call | solution.py:311
  270.8 3.2 collective-permute-start.35
  274.5 3.2 collective-permute-start.37
  277.7 11.9 %expert_mix.7 = (bf16[4,64,2048]{2,1,0:T(8,128)(2,1)S(1)}, bf16[4,64,2048]{2,1,0:T(8,128)(2,1)S(1)}) custom-call(bf16[4,64,2048]{2,1,0:T(8,128)(2,1)} %collective-permute-done.28.xa_ref, bf16[4,64,2048]{2,1,0:T(8,128)(2,1)} %collective-permute-done.31.xb_ref, f32[4,64,2]{2,1,0:T(8,128)S(1)} %get-tuple-element.117.sa_ref, ...), custom_call_target="tpu_custom_call" | custom-call | flops 6442450944 | bytes 16777216 | tf_op jit(solution)/shard_map/expert_mix/pallas_call | solution.py:311
  290.3 3.3 collective-permute-start.39
  294.2 3.3 collective-permute-start.45
  297.5 16.0 %collective-permute-done.38 = bf16[4,64,2048]{2,1,0:T(8,128)(2,1)S(1)} collective-permute-done((bf16[4,64,2048]{2,1,0:T(8,128)(2,1)S(1)}, bf16[4,64,2048]{2,1,0:T(8,128)(2,1)S(1)}, u32[]{:S(2)}, u32[]{:S(2)}) %collective-permute-start.38) | collective-permute-done | bytes 1048608 | tf_op jit(solution)/shard_map/ppermute | solution.py:340
  314.2 3.2 collective-permute-start.42
  318.9 3.2 collective-permute-start.48
  322.4 3.3 collective-permute-start.43
  327.0 2.6 collective-permute-start.49
  330.0 3.9 %collective-permute-done.47 = bf16[64,2048]{1,0:T(8,128)(2,1)S(1)} collective-permute-done((bf16[64,2048]{1,0:T(8,128)(2,1)S(1)}, bf16[64,2048]{1,0:T(8,128)(2,1)S(1)}, u32[]{:S(2)}, u32[]{:S(2)}) %collective-permute-start.47) | collective-permute-done | bytes 262176 | tf_op jit(solution)/shard_map/ppermute | solution.py:340
  (193 shorter events, 60.9 us)
Async XLA Ops:
  6.5 173.1 %all-gather.3.cloned.1.call-start = ((), (), s32[]{:S(2)}) async-start(), calls=%async_computation.1 | async-start | bytes 8912896 | tf_op jit(solution)/shard_map/all_gather | solution.py:461
  9.2 14.0 %collective-permute-start = (bf16[64,2048]{1,0:T(8,128)(2,1)S(1)}, bf16[64,2048]{1,0:T(8,128)(2,1)S(1)}, u32[]{:S(2)}, u32[]{:S(2)}) collective-permute-start(bf16[64,2048]{1,0:T(8,128)(2,1)S(1)} %get-tuple-element.49), channel_id=1, source_target_pairs={{0,3},{1,0},{2,1},{3,2},{4,7},{5,4},{6,5},{7,6},{8,11},{9,8},{10,9... | collective-permute-start | bytes 786440 | tf_op jit(solution)/shard_map/ppermute | solution.py:340
  12.0 12.8 %collective-permute-start.1 = (bf16[64,2048]{1,0:T(8,128)(2,1)S(1)}, bf16[64,2048]{1,0:T(8,128)(2,1)S(1)}, u32[]{:S(2)}, u32[]{:S(2)}) collective-permute-start(bf16[64,2048]{1,0:T(8,128)(2,1)S(1)} %get-tuple-element.49), channel_id=1, source_target_pairs={{0,2},{1,3},{2,0},{3,1},{4,6},{5,7},{6,4},{7,5},{8,10},{9,11},{10,... | collective-permute-start | bytes 786440 | tf_op jit(solution)/shard_map/ppermute | solution.py:340
  12.8 14.1 %collective-permute-start.2 = (bf16[64,2048]{1,0:T(8,128)(2,1)S(1)}, bf16[64,2048]{1,0:T(8,128)(2,1)S(1)}, u32[]{:S(2)}, u32[]{:S(2)}) collective-permute-start(bf16[64,2048]{1,0:T(8,128)(2,1)S(1)} %get-tuple-element.49), channel_id=1, source_target_pairs={{0,1},{1,2},{2,3},{3,0},{4,5},{5,6},{6,7},{7,4},{8,9},{9,10},{10,1... | collective-permute-start | bytes 786440 | tf_op jit(solution)/shard_map/ppermute | solution.py:340
  13.7 13.4 %collective-permute-start.3 = (bf16[64,2048]{1,0:T(8,128)(2,1)S(1)}, bf16[64,2048]{1,0:T(8,128)(2,1)S(1)}, u32[]{:S(2)}, u32[]{:S(2)}) collective-permute-start(bf16[64,2048]{1,0:T(8,128)(2,1)S(1)} %get-tuple-element.53), channel_id=1, source_target_pairs={{0,12},{1,13},{2,14},{3,15},{4,0},{5,1},{6,2},{7,3},{8,4},{9,5},{1... | collective-permute-start | bytes 786440 | tf_op jit(solution)/shard_map/ppermute | solution.py:340
  16.7 10.8 %collective-permute-start.4 = (bf16[64,2048]{1,0:T(8,128)(2,1)S(1)}, bf16[64,2048]{1,0:T(8,128)(2,1)S(1)}, u32[]{:S(2)}, u32[]{:S(2)}) collective-permute-start(bf16[64,2048]{1,0:T(8,128)(2,1)S(1)} %get-tuple-element.53), channel_id=1, source_target_pairs={{0,8},{1,9},{2,10},{3,11},{4,12},{5,13},{6,14},{7,15},{8,0},{9,1},... | collective-permute-start | bytes 786440 | tf_op jit(solution)/shard_map/ppermute | solution.py:340
  23.3 7.6 %collective-permute-start.5 = (bf16[64,2048]{1,0:T(8,128)(2,1)S(1)}, bf16[64,2048]{1,0:T(8,128)(2,1)S(1)}, u32[]{:S(2)}, u32[]{:S(2)}) collective-permute-start(bf16[64,2048]{1,0:T(8,128)(2,1)S(1)} %get-tuple-element.53), channel_id=1, source_target_pairs={{0,4},{1,5},{2,6},{3,7},{4,8},{5,9},{6,10},{7,11},{8,12},{9,13},{1... | collective-permute-start | bytes 786440 | tf_op jit(solution)/shard_map/ppermute | solution.py:340
  31.0 26.1 %collective-permute-start.8 = (bf16[4,64,2048]{2,1,0:T(8,128)(2,1)S(1)}, bf16[4,64,2048]{2,1,0:T(8,128)(2,1)}, u32[]{:S(2)}, u32[]{:S(2)}) collective-permute-start(bf16[4,64,2048]{2,1,0:T(8,128)(2,1)S(1)} %pad_maximum_fusion.1.refs_5_), channel_id=1, source_target_pairs={{0,1},{1,2},{2,3},{3,0},{4,5},{5,6},{6,7},{7,4},{8,9},{9,10},{10,1... | collective-permute-start | bytes 3145736 | tf_op jit(solution)/shard_map/ppermute | solution.py:340
  32.8 24.9 %collective-permute-start.9 = (bf16[4,64,2048]{2,1,0:T(8,128)(2,1)S(1)}, bf16[4,64,2048]{2,1,0:T(8,128)(2,1)}, u32[]{:S(2)}, u32[]{:S(2)}) collective-permute-start(bf16[4,64,2048]{2,1,0:T(8,128)(2,1)S(1)} %pad_maximum_fusion.1.refs_5_), channel_id=1, source_target_pairs={{0,3},{1,0},{2,1},{3,2},{4,7},{5,4},{6,5},{7,6},{8,11},{9,8},{10,9... | collective-permute-start | bytes 3145736 | tf_op jit(solution)/shard_map/ppermute | solution.py:340
  36.8 24.4 %collective-permute-start.6 = (bf16[4,64,2048]{2,1,0:T(8,128)(2,1)}, bf16[4,64,2048]{2,1,0:T(8,128)(2,1)}, u32[]{:S(2)}, u32[]{:S(2)}) collective-permute-start(bf16[4,64,2048]{2,1,0:T(8,128)(2,1)} %pad_maximum_fusion.refs_1_), channel_id=1, source_target_pairs={{0,4},{1,5},{2,6},{3,7},{4,8},{5,9},{6,10},{7,11},{8,12},{9,13},{1... | collective-permute-start | bytes 3145736 | tf_op jit(solution)/shard_map/ppermute | solution.py:340
  37.1 24.1 %collective-permute-start.7 = (bf16[4,64,2048]{2,1,0:T(8,128)(2,1)}, bf16[4,64,2048]{2,1,0:T(8,128)(2,1)}, u32[]{:S(2)}, u32[]{:S(2)}) collective-permute-start(bf16[4,64,2048]{2,1,0:T(8,128)(2,1)} %pad_maximum_fusion.refs_1_), channel_id=1, source_target_pairs={{0,12},{1,13},{2,14},{3,15},{4,0},{5,1},{6,2},{7,3},{8,4},{9,5},{1... | collective-permute-start | bytes 3145736 | tf_op jit(solution)/shard_map/ppermute | solution.py:340
  63.1 13.8 %collective-permute-start.12 = (bf16[2,64,2048]{2,1,0:T(8,128)(2,1)}, bf16[2,64,2048]{2,1,0:T(8,128)(2,1)}, u32[]{:S(2)}, u32[]{:S(2)}) collective-permute-start(bf16[2,64,2048]{2,1,0:T(8,128)(2,1)} %slice.207), channel_id=1, source_target_pairs={{0,1},{1,2},{2,3},{3,0},{4,5},{5,6},{6,7},{7,4},{8,9},{9,10},{10,1... | collective-permute-start | bytes 1572872 | tf_op jit(solution)/shard_map/ppermute | solution.py:340
  65.8 17.6 %collective-permute-start.13 = (bf16[2,64,2048]{2,1,0:T(8,128)(2,1)}, bf16[2,64,2048]{2,1,0:T(8,128)(2,1)}, u32[]{:S(2)}, u32[]{:S(2)}) collective-permute-start(bf16[2,64,2048]{2,1,0:T(8,128)(2,1)} %slice.208), channel_id=1, source_target_pairs={{0,3},{1,0},{2,1},{3,2},{4,7},{5,4},{6,5},{7,6},{8,11},{9,8},{10,9... | collective-permute-start | bytes 1572872 | tf_op jit(solution)/shard_map/ppermute | solution.py:340
  69.3 20.0 %collective-permute-start.10 = (bf16[2,64,2048]{2,1,0:T(8,128)(2,1)S(1)}, bf16[2,64,2048]{2,1,0:T(8,128)(2,1)}, u32[]{:S(2)}, u32[]{:S(2)}) collective-permute-start(bf16[2,64,2048]{2,1,0:T(8,128)(2,1)S(1)} %slice.205), channel_id=1, source_target_pairs={{0,4},{1,5},{2,6},{3,7},{4,8},{5,9},{6,10},{7,11},{8,12},{9,13},{1... | collective-permute-start | bytes 1572872 | tf_op jit(solution)/shard_map/ppermute | solution.py:340
  70.8 19.3 %collective-permute-start.11 = (bf16[2,64,2048]{2,1,0:T(8,128)(2,1)S(1)}, bf16[2,64,2048]{2,1,0:T(8,128)(2,1)}, u32[]{:S(2)}, u32[]{:S(2)}) collective-permute-start(bf16[2,64,2048]{2,1,0:T(8,128)(2,1)S(1)} %slice.206), channel_id=1, source_target_pairs={{0,12},{1,13},{2,14},{3,15},{4,0},{5,1},{6,2},{7,3},{8,4},{9,5},{1... | collective-permute-start | bytes 1572872 | tf_op jit(solution)/shard_map/ppermute | solution.py:340
  130.3 8.5 %collective-permute-start.15 = (bf16[2,128,256]{2,1,0:T(8,128)(2,1)S(1)}, bf16[2,128,256]{2,1,0:T(8,128)(2,1)S(1)}, u32[]{:S(2)}, u32[]{:S(2)}) collective-permute-start(bf16[2,128,256]{2,1,0:T(8,128)(2,1)S(1)} %pad_maximum_fusion.17), channel_id=1, source_target_pairs={{0,96},{16,112},{1,97},{17,113},{2,98},{18,114},{3,99},{19,115},{4... | collective-permute-start | bytes 393224 | tf_op jit(solution)/shard_map/ppermute | solution.py:407
  131.0 9.0 %collective-permute-start.16 = (bf16[2,128,256]{2,1,0:T(8,128)(2,1)S(1)}, bf16[2,128,256]{2,1,0:T(8,128)(2,1)S(1)}, u32[]{:S(2)}, u32[]{:S(2)}) collective-permute-start(bf16[2,128,256]{2,1,0:T(8,128)(2,1)S(1)} %pad_maximum_fusion.17), channel_id=1, source_target_pairs={{0,64},{16,80},{32,96},{48,112},{1,65},{17,81},{33,97},{49,113},{2... | collective-permute-start | bytes 393224 | tf_op jit(solution)/shard_map/ppermute | solution.py:407
  136.9 7.5 %collective-permute-start.17 = (bf16[2,128,256]{2,1,0:T(8,128)(2,1)S(1)}, bf16[2,128,256]{2,1,0:T(8,128)(2,1)S(1)}, u32[]{:S(2)}, u32[]{:S(2)}) collective-permute-start(bf16[2,128,256]{2,1,0:T(8,128)(2,1)S(1)} %pad_maximum_fusion.17), channel_id=1, source_target_pairs={{0,32},{16,48},{32,64},{48,80},{64,96},{80,112},{1,33},{17,49},{33... | collective-permute-start | bytes 393224 | tf_op jit(solution)/shard_map/ppermute | solution.py:407
  188.7 9.2 %collective-permute-start.23 = (bf16[64,2048]{1,0:T(8,128)(2,1)S(1)}, bf16[64,2048]{1,0:T(8,128)(2,1)S(1)}, u32[]{:S(2)}, u32[]{:S(2)}) collective-permute-start(bf16[64,2048]{1,0:T(8,128)(2,1)S(1)} %get-tuple-element.123), channel_id=1, source_target_pairs={{0,12},{1,13},{2,14},{3,15},{4,0},{5,1},{6,2},{7,3},{8,4},{9,5},{1... | collective-permute-start | bytes 786440 | tf_op jit(solution)/shard_map/ppermute | solution.py:340
  191.2 10.7 %collective-permute-start.24 = (bf16[64,2048]{1,0:T(8,128)(2,1)S(1)}, bf16[64,2048]{1,0:T(8,128)(2,1)S(1)}, u32[]{:S(2)}, u32[]{:S(2)}) collective-permute-start(bf16[64,2048]{1,0:T(8,128)(2,1)S(1)} %get-tuple-element.123), channel_id=1, source_target_pairs={{0,8},{1,9},{2,10},{3,11},{4,12},{5,13},{6,14},{7,15},{8,0},{9,1},... | collective-permute-start | bytes 786440 | tf_op jit(solution)/shard_map/ppermute | solution.py:340
  191.8 14.8 %collective-permute-start.25 = (bf16[64,2048]{1,0:T(8,128)(2,1)S(1)}, bf16[64,2048]{1,0:T(8,128)(2,1)S(1)}, u32[]{:S(2)}, u32[]{:S(2)}) collective-permute-start(bf16[64,2048]{1,0:T(8,128)(2,1)S(1)} %get-tuple-element.123), channel_id=1, source_target_pairs={{0,4},{1,5},{2,6},{3,7},{4,8},{5,9},{6,10},{7,11},{8,12},{9,13},{1... | collective-permute-start | bytes 786440 | tf_op jit(solution)/shard_map/ppermute | solution.py:340
  192.6 16.3 %collective-permute-start.20 = (bf16[64,2048]{1,0:T(8,128)(2,1)S(1)}, bf16[64,2048]{1,0:T(8,128)(2,1)S(1)}, u32[]{:S(2)}, u32[]{:S(2)}) collective-permute-start(bf16[64,2048]{1,0:T(8,128)(2,1)S(1)} %get-tuple-element.124), channel_id=1, source_target_pairs={{0,3},{1,0},{2,1},{3,2},{4,7},{5,4},{6,5},{7,6},{8,11},{9,8},{10,9... | collective-permute-start | bytes 786440 | tf_op jit(solution)/shard_map/ppermute | solution.py:340
  193.7 15.1 %collective-permute-start.21 = (bf16[64,2048]{1,0:T(8,128)(2,1)S(1)}, bf16[64,2048]{1,0:T(8,128)(2,1)S(1)}, u32[]{:S(2)}, u32[]{:S(2)}) collective-permute-start(bf16[64,2048]{1,0:T(8,128)(2,1)S(1)} %get-tuple-element.124), channel_id=1, source_target_pairs={{0,2},{1,3},{2,0},{3,1},{4,6},{5,7},{6,4},{7,5},{8,10},{9,11},{10,... | collective-permute-start | bytes 786440 | tf_op jit(solution)/shard_map/ppermute | solution.py:340
  197.8 11.0 %collective-permute-start.22 = (bf16[64,2048]{1,0:T(8,128)(2,1)S(1)}, bf16[64,2048]{1,0:T(8,128)(2,1)S(1)}, u32[]{:S(2)}, u32[]{:S(2)}) collective-permute-start(bf16[64,2048]{1,0:T(8,128)(2,1)S(1)} %get-tuple-element.124), channel_id=1, source_target_pairs={{0,1},{1,2},{2,3},{3,0},{4,5},{5,6},{6,7},{7,4},{8,9},{9,10},{10,1... | collective-permute-start | bytes 786440 | tf_op jit(solution)/shard_map/ppermute | solution.py:340
  206.8 25.3 %collective-permute-start.27 = (bf16[4,64,2048]{2,1,0:T(8,128)(2,1)S(1)}, bf16[4,64,2048]{2,1,0:T(8,128)(2,1)}, u32[]{:S(2)}, u32[]{:S(2)}) collective-permute-start(bf16[4,64,2048]{2,1,0:T(8,128)(2,1)S(1)} %pad_maximum_fusion.5.xb_ref), channel_id=1, source_target_pairs={{0,3},{1,0},{2,1},{3,2},{4,7},{5,4},{6,5},{7,6},{8,11},{9,8},{10,9... | collective-permute-start | bytes 3145736 | tf_op jit(solution)/shard_map/ppermute | solution.py:340
  207.7 27.6 %collective-permute-start.31 = (bf16[4,64,2048]{2,1,0:T(8,128)(2,1)S(1)}, bf16[4,64,2048]{2,1,0:T(8,128)(2,1)}, u32[]{:S(2)}, u32[]{:S(2)}) collective-permute-start(bf16[4,64,2048]{2,1,0:T(8,128)(2,1)S(1)} %pad_maximum_fusion.5.xb_ref), channel_id=1, source_target_pairs={{0,1},{1,2},{2,3},{3,0},{4,5},{5,6},{6,7},{7,4},{8,9},{9,10},{10,1... | collective-permute-start | bytes 3145736 | tf_op jit(solution)/shard_map/ppermute | solution.py:340
  210.0 25.3 %collective-permute-start.26 = (bf16[4,64,2048]{2,1,0:T(8,128)(2,1)}, bf16[4,64,2048]{2,1,0:T(8,128)(2,1)}, u32[]{:S(2)}, u32[]{:S(2)}) collective-permute-start(bf16[4,64,2048]{2,1,0:T(8,128)(2,1)} %pad_maximum_fusion.4.xa_ref), channel_id=1, source_target_pairs={{0,12},{1,13},{2,14},{3,15},{4,0},{5,1},{6,2},{7,3},{8,4},{9,5},{1... | collective-permute-start | bytes 3145736 | tf_op jit(solution)/shard_map/ppermute | solution.py:340
  212.5 28.5 %collective-permute-start.28 = (bf16[4,64,2048]{2,1,0:T(8,128)(2,1)}, bf16[4,64,2048]{2,1,0:T(8,128)(2,1)}, u32[]{:S(2)}, u32[]{:S(2)}) collective-permute-start(bf16[4,64,2048]{2,1,0:T(8,128)(2,1)} %pad_maximum_fusion.4.xa_ref), channel_id=1, source_target_pairs={{0,4},{1,5},{2,6},{3,7},{4,8},{5,9},{6,10},{7,11},{8,12},{9,13},{1... | collective-permute-start | bytes 3145736 | tf_op jit(solution)/shard_map/ppermute | solution.py:340
  236.5 22.4 %collective-permute-start.32 = (bf16[2,64,2048]{2,1,0:T(8,128)(2,1)S(1)}, bf16[2,64,2048]{2,1,0:T(8,128)(2,1)S(1)}, u32[]{:S(2)}, u32[]{:S(2)}) collective-permute-start(bf16[2,64,2048]{2,1,0:T(8,128)(2,1)S(1)} %slice.277), channel_id=1, source_target_pairs={{0,1},{1,2},{2,3},{3,0},{4,5},{5,6},{6,7},{7,4},{8,9},{9,10},{10,1... | collective-permute-start | bytes 1572872 | tf_op jit(solution)/shard_map/ppermute | solution.py:340
  237.8 21.1 %collective-permute-start.33 = (bf16[2,64,2048]{2,1,0:T(8,128)(2,1)S(1)}, bf16[2,64,2048]{2,1,0:T(8,128)(2,1)S(1)}, u32[]{:S(2)}, u32[]{:S(2)}) collective-permute-start(bf16[2,64,2048]{2,1,0:T(8,128)(2,1)S(1)} %slice.278), channel_id=1, source_target_pairs={{0,3},{1,0},{2,1},{3,2},{4,7},{5,4},{6,5},{7,6},{8,11},{9,8},{10,9... | collective-permute-start | bytes 1572872 | tf_op jit(solution)/shard_map/ppermute | solution.py:340
  242.0 16.9 %collective-permute-start.29 = (bf16[2,64,2048]{2,1,0:T(8,128)(2,1)S(1)}, bf16[2,64,2048]{2,1,0:T(8,128)(2,1)S(1)}, u32[]{:S(2)}, u32[]{:S(2)}) collective-permute-start(bf16[2,64,2048]{2,1,0:T(8,128)(2,1)S(1)} %slice.275), channel_id=1, source_target_pairs={{0,4},{1,5},{2,6},{3,7},{4,8},{5,9},{6,10},{7,11},{8,12},{9,13},{1... | collective-permute-start | bytes 1572872 | tf_op jit(solution)/shard_map/ppermute | solution.py:340
  244.5 14.4 %collective-permute-start.30 = (bf16[2,64,2048]{2,1,0:T(8,128)(2,1)S(1)}, bf16[2,64,2048]{2,1,0:T(8,128)(2,1)S(1)}, u32[]{:S(2)}, u32[]{:S(2)}) collective-permute-start(bf16[2,64,2048]{2,1,0:T(8,128)(2,1)S(1)} %slice.276), channel_id=1, source_target_pairs={{0,12},{1,13},{2,14},{3,15},{4,0},{5,1},{6,2},{7,3},{8,4},{9,5},{1... | collective-permute-start | bytes 1572872 | tf_op jit(solution)/shard_map/ppermute | solution.py:340
  270.7 19.0 %collective-permute-start.34 = (bf16[2,64,2048]{2,1,0:T(8,128)(2,1)S(1)}, bf16[2,64,2048]{2,1,0:T(8,128)(2,1)S(1)}, u32[]{:S(2)}, u32[]{:S(2)}) collective-permute-start(bf16[2,64,2048]{2,1,0:T(8,128)(2,1)S(1)} %get-tuple-element.108), channel_id=1, source_target_pairs={{0,4},{1,5},{2,6},{3,7},{4,8},{5,9},{6,10},{7,11},{8,12},{9,13},{1... | collective-permute-start | bytes 1572872 | tf_op jit(solution)/shard_map/ppermute | solution.py:340
  270.8 19.0 %collective-permute-start.35 = (bf16[2,64,2048]{2,1,0:T(8,128)(2,1)S(1)}, bf16[2,64,2048]{2,1,0:T(8,128)(2,1)S(1)}, u32[]{:S(2)}, u32[]{:S(2)}) collective-permute-start(bf16[2,64,2048]{2,1,0:T(8,128)(2,1)S(1)} %get-tuple-element.107), channel_id=1, source_target_pairs={{0,12},{1,13},{2,14},{3,15},{4,0},{5,1},{6,2},{7,3},{8,4},{9,5},{1... | collective-permute-start | bytes 1572872 | tf_op jit(solution)/shard_map/ppermute | solution.py:340
  274.1 15.7 %collective-permute-start.36 = (bf16[2,64,2048]{2,1,0:T(8,128)(2,1)S(1)}, bf16[2,64,2048]{2,1,0:T(8,128)(2,1)S(1)}, u32[]{:S(2)}, u32[]{:S(2)}) collective-permute-start(bf16[2,64,2048]{2,1,0:T(8,128)(2,1)S(1)} %get-tuple-element.106), channel_id=1, source_target_pairs={{0,1},{1,2},{2,3},{3,0},{4,5},{5,6},{6,7},{7,4},{8,9},{9,10},{10,1... | collective-permute-start | bytes 1572872 | tf_op jit(solution)/shard_map/ppermute | solution.py:340
  274.5 15.3 %collective-permute-start.37 = (bf16[2,64,2048]{2,1,0:T(8,128)(2,1)S(1)}, bf16[2,64,2048]{2,1,0:T(8,128)(2,1)S(1)}, u32[]{:S(2)}, u32[]{:S(2)}) collective-permute-start(bf16[2,64,2048]{2,1,0:T(8,128)(2,1)S(1)} %get-tuple-element.105), channel_id=1, source_target_pairs={{0,3},{1,0},{2,1},{3,2},{4,7},{5,4},{6,5},{7,6},{8,11},{9,8},{10,9... | collective-permute-start | bytes 1572872 | tf_op jit(solution)/shard_map/ppermute | solution.py:340
  290.0 23.5 %collective-permute-start.38 = (bf16[4,64,2048]{2,1,0:T(8,128)(2,1)S(1)}, bf16[4,64,2048]{2,1,0:T(8,128)(2,1)S(1)}, u32[]{:S(2)}, u32[]{:S(2)}) collective-permute-start(bf16[4,64,2048]{2,1,0:T(8,128)(2,1)S(1)} %pad_maximum_fusion.8), channel_id=1, source_target_pairs={{0,4},{1,5},{2,6},{3,7},{4,8},{5,9},{6,10},{7,11},{8,12},{9,13},{1... | collective-permute-start | bytes 3145736 | tf_op jit(solution)/shard_map/ppermute | solution.py:340
  290.3 23.2 %collective-permute-start.39 = (bf16[4,64,2048]{2,1,0:T(8,128)(2,1)S(1)}, bf16[4,64,2048]{2,1,0:T(8,128)(2,1)S(1)}, u32[]{:S(2)}, u32[]{:S(2)}) collective-permute-start(bf16[4,64,2048]{2,1,0:T(8,128)(2,1)S(1)} %pad_maximum_fusion.9), channel_id=1, source_target_pairs={{0,12},{1,13},{2,14},{3,15},{4,0},{5,1},{6,2},{7,3},{8,4},{9,5},{1... | collective-permute-start | bytes 3145736 | tf_op jit(solution)/shard_map/ppermute | solution.py:340
  293.9 24.3 %collective-permute-start.44 = (bf16[4,64,2048]{2,1,0:T(8,128)(2,1)S(1)}, bf16[4,64,2048]{2,1,0:T(8,128)(2,1)S(1)}, u32[]{:S(2)}, u32[]{:S(2)}) collective-permute-start(bf16[4,64,2048]{2,1,0:T(8,128)(2,1)S(1)} %pad_maximum_fusion.10), channel_id=1, source_target_pairs={{0,1},{1,2},{2,3},{3,0},{4,5},{5,6},{6,7},{7,4},{8,9},{9,10},{10,1... | collective-permute-start | bytes 3145736 | tf_op jit(solution)/shard_map/ppermute | solution.py:340
  294.2 24.0 %collective-permute-start.45 = (bf16[4,64,2048]{2,1,0:T(8,128)(2,1)S(1)}, bf16[4,64,2048]{2,1,0:T(8,128)(2,1)S(1)}, u32[]{:S(2)}, u32[]{:S(2)}) collective-permute-start(bf16[4,64,2048]{2,1,0:T(8,128)(2,1)S(1)} %pad_maximum_fusion.11), channel_id=1, source_target_pairs={{0,3},{1,0},{2,1},{3,2},{4,7},{5,4},{6,5},{7,6},{8,11},{9,8},{10,9... | collective-permute-start | bytes 3145736 | tf_op jit(solution)/shard_map/ppermute | solution.py:340
  314.1 8.0 %collective-permute-start.40 = (bf16[32,2048]{1,0:T(8,128)(2,1)S(1)}, bf16[32,2048]{1,0:T(8,128)(2,1)S(1)}, u32[]{:S(2)}, u32[]{:S(2)}) collective-permute-start(bf16[32,2048]{1,0:T(8,128)(2,1)S(1)} %get-tuple-element.95), channel_id=1, source_target_pairs={{0,1},{1,2},{2,3},{3,0},{4,5},{5,6},{6,7},{7,4},{8,9},{9,10},{10,1... | collective-permute-start | bytes 393224 | tf_op jit(solution)/shard_map/ppermute | solution.py:340
  314.2 7.9 %collective-permute-start.42 = (bf16[32,2048]{1,0:T(8,128)(2,1)S(1)}, bf16[32,2048]{1,0:T(8,128)(2,1)S(1)}, u32[]{:S(2)}, u32[]{:S(2)}) collective-permute-start(bf16[32,2048]{1,0:T(8,128)(2,1)S(1)} %get-tuple-element.96), channel_id=1, source_target_pairs={{0,3},{1,0},{2,1},{3,2},{4,7},{5,4},{6,5},{7,6},{8,11},{9,8},{10,9... | collective-permute-start | bytes 393224 | tf_op jit(solution)/shard_map/ppermute | solution.py:340
  318.8 7.2 %collective-permute-start.46 = (bf16[32,2048]{1,0:T(8,128)(2,1)S(1)}, bf16[32,2048]{1,0:T(8,128)(2,1)S(1)}, u32[]{:S(2)}, u32[]{:S(2)}) collective-permute-start(bf16[32,2048]{1,0:T(8,128)(2,1)S(1)} %get-tuple-element.101), channel_id=1, source_target_pairs={{0,4},{1,5},{2,6},{3,7},{4,8},{5,9},{6,10},{7,11},{8,12},{9,13},{1... | collective-permute-start | bytes 393224 | tf_op jit(solution)/shard_map/ppermute | solution.py:340
  318.9 7.1 %collective-permute-start.48 = (bf16[32,2048]{1,0:T(8,128)(2,1)S(1)}, bf16[32,2048]{1,0:T(8,128)(2,1)S(1)}, u32[]{:S(2)}, u32[]{:S(2)}) collective-permute-start(bf16[32,2048]{1,0:T(8,128)(2,1)S(1)} %get-tuple-element.102), channel_id=1, source_target_pairs={{0,12},{1,13},{2,14},{3,15},{4,0},{5,1},{6,2},{7,3},{8,4},{9,5},{1... | collective-permute-start | bytes 393224 | tf_op jit(solution)/shard_map/ppermute | solution.py:340
  322.2 7.7 %collective-permute-start.41 = (bf16[64,2048]{1,0:T(8,128)(2,1)S(1)}, bf16[64,2048]{1,0:T(8,128)(2,1)S(1)}, u32[]{:S(2)}, u32[]{:S(2)}) collective-permute-start(bf16[64,2048]{1,0:T(8,128)(2,1)S(1)} %pad_maximum_fusion.13), channel_id=1, source_target_pairs={{0,1},{1,2},{2,3},{3,0},{4,5},{5,6},{6,7},{7,4},{8,9},{9,10},{10,1... | collective-permute-start | bytes 786440 | tf_op jit(solution)/shard_map/ppermute | solution.py:340
  322.4 7.5 %collective-permute-start.43 = (bf16[64,2048]{1,0:T(8,128)(2,1)S(1)}, bf16[64,2048]{1,0:T(8,128)(2,1)S(1)}, u32[]{:S(2)}, u32[]{:S(2)}) collective-permute-start(bf16[64,2048]{1,0:T(8,128)(2,1)S(1)} %pad_maximum_fusion.14), channel_id=1, source_target_pairs={{0,3},{1,0},{2,1},{3,2},{4,7},{5,4},{6,5},{7,6},{8,11},{9,8},{10,9... | collective-permute-start | bytes 786440 | tf_op jit(solution)/shard_map/ppermute | solution.py:340
  326.1 7.8 %collective-permute-start.47 = (bf16[64,2048]{1,0:T(8,128)(2,1)S(1)}, bf16[64,2048]{1,0:T(8,128)(2,1)S(1)}, u32[]{:S(2)}, u32[]{:S(2)}) collective-permute-start(bf16[64,2048]{1,0:T(8,128)(2,1)S(1)} %pad_maximum_fusion.15), channel_id=1, source_target_pairs={{0,4},{1,5},{2,6},{3,7},{4,8},{5,9},{6,10},{7,11},{8,12},{9,13},{1... | collective-permute-start | bytes 786440 | tf_op jit(solution)/shard_map/ppermute | solution.py:340
  327.0 6.9 %collective-permute-start.49 = (bf16[64,2048]{1,0:T(8,128)(2,1)S(1)}, bf16[64,2048]{1,0:T(8,128)(2,1)S(1)}, u32[]{:S(2)}, u32[]{:S(2)}) collective-permute-start(bf16[64,2048]{1,0:T(8,128)(2,1)S(1)} %pad_maximum_fusion.16), channel_id=1, source_target_pairs={{0,12},{1,13},{2,14},{3,15},{4,0},{5,1},{6,2},{7,3},{8,4},{9,5},{1... | collective-permute-start | bytes 786440 | tf_op jit(solution)/shard_map/ppermute | solution.py:340
  (29 other events, 444.6 us)
Sparse Core Ops, SparseCore 0:
  61.3 74.3 all-gather.2
where the time goes:
time: 350 us; the launch traced here: 343 us
  Pallas kernels  87.2 us (25%)
  waiting for transfers between devices  85.6 us (24%)
  starting transfers between devices  78.7 us (22%)
  blocking collectives  22.9 us (7%)
  local copies, waits for them, and re-layouts  21.9 us (6%)
  other arithmetic  20.3 us (6%)
  between operations  14.7 us (4%)
  matrix products  11.6 us (3%)
    ppermute x44, waiting for transfers between devices, neighbour(): return lax.ppermute(value, 'exp', pairs)  78.7 us
    ppermute x44, starting transfers between devices, neighbour(): return lax.ppermute(value, 'exp', pairs)  69.4 us
    pallas_call x4, Pallas kernels, expert_mix(): pl.pallas_call(expert_kernel, grid=(count * EXPERT_CUTS,), in_specs=[rows...  46.1 us
    pallas_call x1, Pallas kernels, delta_local(): pl.pallas_call(lambda *refs: delta_kernel(blocks, *refs), grid_spec=pltpu...  34.3 us
    all_to_all x1, blocking collectives, local(): lax.all_to_all(gated.reshape(owners, tok_dev, -1), 'exp', split_axis=0, c...  22.9 us
    ppermute x6, starting transfers between devices, along_seq(): return lax.ppermute(value, 'seq', pairs)  9.24 us
  transfers between devices with their start and end apart: 51, of which 25 were waited for; matrix products, arithmetic and copies ran while one was open for 11% of the time, Pallas kernels for 22%

commit v1 on v0

--- a/solution.py
+++ b/solution.py
@@ -53,24 +53,28 @@
     place_ref,
     *refs,
 ):
-    gathered, refs = refs[: 2 * SIDE], refs[2 * SIDE :]
+    gathered, refs = refs[: 4 * SIDE], refs[4 * SIDE :]
     query_ref, key_ref, value_ref, outgate_ref, cum_ref, rate_ref = refs[:6]
-    base_ref, reach_ref, gate_ref, total_ref, state, held, lines, proj_ref, arrived = refs[6:]
+    base_ref, reach_ref, gate_ref, total_ref, state, held, lines, proj_ref, pair_ref, arrived = refs[6:]
     step = pl.program_id(0)
 
     @pl.when(step == 0)
     def _():
         copies = [
-            pltpu.make_async_copy(ref, held.at[i // SIDE, i % SIDE], arrived.at[i])
+            pltpu.make_async_copy(
+                ref, held.at[i // (2 * SIDE), i // 2 % SIDE, pl.ds(i % 2 * 2, 2)], arrived.at[i]
+            )
             for i, ref in enumerate(gathered)
         ]
         for copy in copies:
             copy.start()
+        pair_ref[:, :DK] = query_ref[...]
+        pair_ref[:, DK:] = key_ref[...]
         for copy in copies:
             copy.wait()
 
     part = held.shape[3]
-    pair = 2
+    pair = 4
 
     def project(c, carry):
         for u in range(pair):
@@ -81,8 +85,7 @@
             lines[u * BLOCK + part : (u + 1) * BLOCK] = held[1, far_x, far_y]
         x = lines[...]
         span = pl.ds(pl.multiple_of(c * pair * BLOCK, pair * BLOCK), pair * BLOCK)
-        proj_ref[span, 0:DK] = mm(x, query_ref[...])
-        proj_ref[span, DK : 2 * DK] = mm(x, key_ref[...])
+        proj_ref[span, : 2 * DK] = mm(x, pair_ref[...])
         proj_ref[span, 2 * DK :] = mm(x, value_ref[...])
         gate_ref[span, :] = mm(x, outgate_ref[...])
         return carry
@@ -170,7 +173,9 @@
 
 
 def delta_local(place, firsts, seconds, weights, cumulative, rates):
-    side, part, width = firsts[0].shape
+    pieces = [piece for pair in firsts + seconds for piece in pair]
+    side = SIDE
+    _, part, width = pieces[0].shape
     tokens = 2 * side * side * part
     blocks = 8
     whole = lambda i, p: (0, 0)
@@ -181,7 +186,7 @@
         grid_spec=pltpu.PrefetchScalarGridSpec(
             num_scalar_prefetch=1,
             grid=(tokens // (blocks * BLOCK),),
-            in_specs=[pl.BlockSpec(memory_space=pl.ANY)] * (2 * side)
+            in_specs=[pl.BlockSpec(memory_space=pl.ANY)] * (4 * side)
             + [pl.BlockSpec(w.shape, whole, pipeline_mode=pl.Buffered(1)) for w in weights]
             + [rates_spec, rates_spec],
             out_specs=[
@@ -193,9 +198,10 @@
             scratch_shapes=[
                 pltpu.VMEM((2, DK, DK + DV), F32),
                 pltpu.VMEM((2, side, side, part, width), BF16),
-                pltpu.VMEM((2 * BLOCK, width), BF16),
+                pltpu.VMEM((4 * BLOCK, width), BF16),
                 pltpu.VMEM((blocks * BLOCK, 2 * DK + 2 * DV), F32),
-                pltpu.SemaphoreType.DMA((2 * side,)),
+                pltpu.VMEM((width, 2 * DK), BF16),
+                pltpu.SemaphoreType.DMA((4 * side,)),
             ],
         ),
         out_shape=[jax.ShapeDtypeStruct((tokens, 2 * DV), F32)] * 3
@@ -205,7 +211,7 @@
             flops=3 * 10**10, bytes_accessed=2 * 10**7, transcendentals=0
         ),
         name="delta_local",
-    )(place, *firsts, *seconds, *weights, cumulative, rates)
+    )(place, *pieces, *weights, cumulative, rates)
 
 
 def gate_kernel(
@@ -259,20 +265,22 @@
     )(place, maps, base, reach, gate, gain)
 
 
-def expert_kernel(xa_ref, xb_ref, sa_ref, sb_ref, gate_ref, up_ref, down_ref, oa_ref, ob_ref, x_ref, total):
-    width = xa_ref.shape[-1]
-    rows = xa_ref.size // width
+def expert_kernel(*refs):
+    pieces, (sa_ref, sb_ref, gate_ref, up_ref, down_ref), outs = refs[:4], refs[4:9], refs[9:13]
+    x_ref, total = refs[13:]
+    width = x_ref.shape[1]
+    rows = x_ref.shape[0] // 4
     step = pl.program_id(0)
     expert = step // EXPERT_CUTS
 
     @pl.when(step == 0)
     def _():
-        x_ref[:rows] = xa_ref[...].reshape(rows, width)
-        x_ref[rows:] = xb_ref[...].reshape(rows, width)
+        for i, piece in enumerate(pieces):
+            x_ref[i * rows : (i + 1) * rows] = piece[...].reshape(rows, width)
 
     x = x_ref[...]
     shares = jnp.concatenate(
-        [sa_ref[...].reshape(rows, -1), sb_ref[...].reshape(rows, -1)], axis=0
+        [sa_ref[...].reshape(2 * rows, -1), sb_ref[...].reshape(2 * rows, -1)], axis=0
     )
     share = jnp.where(expert == 0, shares[:, 0:1], shares[:, 1:2])
     gated = mm(x, gate_ref[0])
@@ -290,30 +298,32 @@
 
     @pl.when(step == pl.num_programs(0) - 1)
     def _():
-        done = (total[...] + made).astype(oa_ref.dtype)
-        oa_ref[...] = done[:rows].reshape(oa_ref.shape)
-        ob_ref[...] = done[rows:].reshape(ob_ref.shape)
+        done = (total[...] + made).astype(outs[0].dtype)
+        for i, out in enumerate(outs):
+            out[...] = done[i * rows : (i + 1) * rows].reshape(out.shape)
 
 
 EXPERT_CUTS = 2
 
 
 def expert_mix(xa, xb, sa, sb, w_gate, w_up, w_down):
-    side, part, width = xa.shape
+    pieces = (*xa, *xb)
+    _, part, width = pieces[0].shape
+    side = SIDE
     count, _, inner = w_gate.shape
     cut = inner // EXPERT_CUTS
     whole = lambda i: (0, 0, 0)
-    rows_spec = pl.BlockSpec((side, part, width), whole, pipeline_mode=pl.Buffered(1))
+    rows_spec = pl.BlockSpec((2, part, width), whole, pipeline_mode=pl.Buffered(1))
     share_spec = pl.BlockSpec((side, part, count), whole, pipeline_mode=pl.Buffered(1))
-    out_spec = pl.BlockSpec((side, part, width), whole)
+    out_spec = pl.BlockSpec((2, part, width), whole)
     across = pl.BlockSpec((1, width, cut), lambda i: (i // EXPERT_CUTS, 0, i % EXPERT_CUTS))
     down = pl.BlockSpec((1, cut, width), lambda i: (i // EXPERT_CUTS, i % EXPERT_CUTS, 0))
     return pl.pallas_call(
         expert_kernel,
         grid=(count * EXPERT_CUTS,),
-        in_specs=[rows_spec, rows_spec, share_spec, share_spec, across, across, down],
-        out_specs=[out_spec, out_spec],
-        out_shape=[jax.ShapeDtypeStruct((side, part, width), BF16)] * 2,
+        in_specs=[rows_spec] * 4 + [share_spec, share_spec, across, across, down],
+        out_specs=[out_spec] * 4,
+        out_shape=[jax.ShapeDtypeStruct((2, part, width), BF16)] * 4,
         scratch_shapes=[
             pltpu.VMEM((2 * side * part, width), BF16),
             pltpu.VMEM((2 * side * part, width), F32),
@@ -325,7 +335,7 @@
             transcendentals=2 * side * part * count * inner,
         ),
         name="expert_mix",
-    )(xa, xb, sa, sb, w_gate, w_up, w_down)
+    )(*pieces, sa, sb, w_gate, w_up, w_down)
 
 
 SIDE = 4
@@ -348,59 +358,60 @@
 
 
 def far_sums(groups, axis):
-    far = groups(2)
-    half = far.shape[0] // 2
-    return neighbour(far[:half], axis, 1), neighbour(far[half:], axis, -1)
-
-
-def near_sums(groups, axis, up, down, final):
-    half = up.shape[0]
-    ahead, behind = groups(1), groups(-1)
-    ahead = jnp.concatenate([plus(ahead[:half], up).astype(BF16), ahead[half:]], axis=0)
-    behind = jnp.concatenate([behind[:half], plus(behind[half:], down).astype(BF16)], axis=0)
-    from_behind = neighbour(ahead, axis, 1)
-    from_ahead = neighbour(behind, axis, -1)
-    return plus(groups(0), from_behind, from_ahead).astype(final)
+    early, late = groups(2)
+    return neighbour(early, axis, 1), neighbour(late, axis, -1)
+
+
+def near_sums(groups, axis, up, down):
+    own, ahead, behind = groups(0), groups(1), groups(-1)
+    behind_late = neighbour(ahead[1], axis, 1)
+    ahead_early = neighbour(behind[0], axis, -1)
+    behind_early = neighbour(plus(ahead[0], up).astype(BF16), axis, 1)
+    ahead_late = neighbour(plus(behind[1], down).astype(BF16), axis, -1)
+    return (
+        plus(own[0], behind_early, ahead_early).astype(BF16),
+        plus(own[1], behind_late, ahead_late).astype(BF16),
+    )
+
+
+def direct_sums(pair, axis):
+    terms = [pair[0][0], pair[0][1], pair[1][0], pair[1][1]]
+    far = neighbour(terms[2], axis, 2)
+    behind = neighbour(terms[1], axis, 1)
+    ahead = neighbour(terms[3], axis, -1)
+    return plus(terms[0], behind, ahead, far)
 
 
 def scatter_sums(first, second):
     up_a, down_a = far_sums(first, 0)
     up_b, down_b = far_sums(second, 1)
     up_a, down_a, up_b, down_b = lax.optimization_barrier((up_a, down_a, up_b, down_b))
-    a = near_sums(first, 0, up_a, down_a, BF16)
-    b = near_sums(second, 1, up_b, down_b, BF16)
-    first, second = (lambda k: a[k % SIDE]), (lambda k: b[k % SIDE])
-    a_last = near_sums(first, 1, *far_sums(first, 1), F32)
-    b_last = near_sums(second, 0, *far_sums(second, 0), F32)
-    return jnp.concatenate([a_last, b_last], axis=0)
+    a = near_sums(first, 0, up_a, down_a)
+    b = near_sums(second, 1, up_b, down_b)
+    return jnp.concatenate([direct_sums(a, 1), direct_sums(b, 0)], axis=0)
 
 
 def gather_direct(block, axis):
-    return [
-        block,
-        neighbour(block, axis, -1),
-        neighbour(block, axis, 2),
-        neighbour(block, axis, 1),
-    ]
+    ahead, far, behind = (neighbour(block, axis, by) for by in (-1, 2, 1))
+    return jnp.stack([block, ahead]), jnp.stack([far, behind])
+
+
+def gather_pieces(pair, axis):
+    early, late = pair
+    behind_early = neighbour(early, axis, 1)
+    ahead_late = neighbour(late, axis, -1)
+    behind_late = neighbour(late, axis, 1)
+    ahead_early = neighbour(early, axis, -1)
+    far = (neighbour(behind_early, axis, 1), neighbour(ahead_late, axis, -1))
+    return [pair, (ahead_early, ahead_late), far, (behind_early, behind_late)]
 
 
 def gather_rows(rows, beside=None):
-    tie = (lambda v: v) if beside is None else lax.optimization_barrier
     part = rows.shape[0] // 2
     a, b = gather_direct(rows[:part], 1), gather_direct(rows[part:], 0)
-    a, b = tie((a, b))
-    a, b = jnp.stack(a), jnp.stack(b)
-    half = a.shape[0] // 2
-    a_behind, a_ahead = neighbour(a, 0, 1), neighbour(a, 0, -1)
-    b_behind, b_ahead = neighbour(b, 1, 1), neighbour(b, 1, -1)
-    a_behind, a_ahead, b_behind, b_ahead, beside = tie(
-        (a_behind, a_ahead, b_behind, b_ahead, beside)
-    )
-    a_far = (neighbour(a_behind[:half], 0, 1), neighbour(a_ahead[half:], 0, -1))
-    b_far = (neighbour(b_behind[:half], 1, 1), neighbour(b_ahead[half:], 1, -1))
-    first = [a, a_ahead, jnp.concatenate(a_far, axis=0), a_behind]
-    second = [b, b_ahead, jnp.concatenate(b_far, axis=0), b_behind]
-    return first, second, beside
+    if beside is not None:
+        a, b, beside = lax.optimization_barrier((a, b, beside))
+    return gather_pieces(a, 0), gather_pieces(b, 1), beside
 
 
 def along_seq(value, pairs):
@@ -455,10 +466,15 @@
     y, x = position // SIDE, position % SIDE
     core = lax.axis_index("seq") % 2
     place = jnp.stack([y, x, core]).astype(jnp.int32)
-    half = w_output.shape[1] // 2
-    w_half = lax.dynamic_slice_in_dim(w_output, core * half, half, 1)
-    firsts, seconds, w_half = gather_rows(normed, w_half)
-    w_half = lax.all_gather(w_half, "exp", axis=0)
+    chips = lax.axis_size("seq") // 2
+    piece = w_output.shape[1] // (2 * chips)
+    w_piece = lax.dynamic_slice_in_dim(
+        w_output, (core * chips + lax.axis_index("seq") // 2) * piece, piece, 1
+    )
+    w_piece = lax.all_gather(w_piece, "exp", axis=0, tiled=True)
+    firsts, seconds, w_piece = gather_rows(normed, w_piece)
+    same_core = [[2 * i + c for i in range(chips)] for c in range(2)]
+    w_half = lax.all_gather(w_piece, "seq", axis=0, axis_index_groups=same_core)
     blocks = tok_seq // BLOCK
     cumulative = jnp.cumsum(log_decay.reshape(2, blocks, BLOCK), axis=-1)
     weights = (w_query, w_key, w_value, w_outgate)
@@ -471,7 +487,13 @@
         gated.reshape(owners, tok_dev, -1), "exp", split_axis=0, concat_axis=0, tiled=True
     )
     theirs = other_core(arrived)
-    mix = lambda rows: jnp.einsum("stc,scd->td", rows, w_half, preferred_element_type=F32)
+
+    def mix(rows):
+        rows = jnp.transpose(rows, (1, 0, 2)).reshape(tok_dev, -1)
+        return jnp.concatenate(
+            [jnp.dot(rows, w_half[i], preferred_element_type=F32) for i in range(chips)], axis=1
+        )
+
     back = other_core(mix(theirs).astype(BF16)).astype(F32)
     kept = mix(arrived)
     mixed_out = jnp.concatenate(
@@ -495,16 +517,17 @@
     share_first = jnp.transpose(shares[:, :, :, 0], (1, 2, 3, 0))
     share_second = jnp.transpose(shares[:, :, :, 1], (2, 1, 3, 0))
     made = {}
-    previous = None
+    previous = shared
     for k in (0, 1, 2, 3):
         xa, xb = rows_first[k], rows_second[k]
-        if previous is None:
-            xa, xb, shared = lax.optimization_barrier((xa, xb, shared))
+        xa, xb, previous = lax.optimization_barrier((xa, xb, previous))
+        if k == 0:
+            shared = previous
         else:
-            xa, xb, *made[previous] = lax.optimization_barrier((xa, xb, *made[previous]))
-        made[k] = expert_mix(xa, xb, share_first[k], share_second[k], w_gate, w_up, w_down)
-        previous = k
-    routed = scatter_sums(lambda k: made[k % SIDE][0], lambda k: made[k % SIDE][1])
+            made[k - 1] = previous
+        previous = expert_mix(xa, xb, share_first[k], share_second[k], w_gate, w_up, w_down)
+    made[3] = previous
+    routed = scatter_sums(lambda k: made[k % SIDE][:2], lambda k: made[k % SIDE][2:])
     return (residual + shared + routed).astype(BF16)
 
 

time: 350 us -> 373 us (1.066)
  waiting for transfers between devices: 85.6 us -> 147 us
  blocking collectives: 22.9 us -> 0 us
  local copies, waits for them, and re-layouts: 21.9 us -> 8.17 us
  matrix products: 11.6 us -> 22.1 us
  Pallas kernels: 87.2 us -> 82.1 us
  other arithmetic: 20.3 us -> 16.2 us
    all_gather x1 -> x2, waiting for transfers between devices: 0.01 us -> 23.8 us  [the longest x1 23.8 us: local(): w_piece = lax.all_gather(w_piece, 'exp', axis=0, tiled=True)]
    all_to_all x1 -> x0, blocking collectives: 22.9 us -> none  [local(): lax.all_to_all(gated.reshape(owners, tok_dev, -1), 'exp', split_axis=0, c...]
    ppermute x44 -> x54, waiting for transfers between devices: 78.7 us -> 97 us  [neighbour(): return lax.ppermute(value, 'exp', pairs)]
    all_to_all x0 -> x1, waiting for transfers between devices: none -> 17.4 us  [local(): lax.all_to_all(gated.reshape(owners, tok_dev, -1), 'exp', split_axis=0, c...]
    slice x17 -> x0, local copies, waits for them, and re-layouts: 10.8 us -> none  [the longest x4 6 us: gather_rows(): b_far = (neighbour(b_behind[:half], 1, 1), neighbour(b_ahead[half:], 1, -1))]
    dot_general x2 -> x8, matrix products: 6.45 us -> 16.9 us  [mix(): jnp.dot(rows, w_half[i], preferred_element_type=F32)]
    concatenate x12 -> x1, other arithmetic: 5.22 us -> 0.02 us  [mix(): jnp.concatenate([jnp.dot(rows, w_half[i], preferred_element_type=F32) for...]
    ppermute x44 -> x54, starting transfers between devices: 69.4 us -> 64.6 us  [neighbour(): return lax.ppermute(value, 'exp', pairs)]
  transfers between devices with their start and end apart: 51 -> 63, of which waited for: 25 -> 29; matrix products, arithmetic and copies ran while one was open for 11% -> 8% of each run, Pallas kernels for 22% -> 22%
where the time goes in v1:
time: 373 us; the launch traced here: 367 us
  waiting for transfers between devices  147 us (39%)
  Pallas kernels  82.1 us (22%)
  starting transfers between devices  76.9 us (21%)
  matrix products  22.1 us (6%)
  other arithmetic  16.2 us (4%)
  between operations  14.7 us (4%)
  local copies, waits for them, and re-layouts  8.17 us (2%)
    ppermute x54, waiting for transfers between devices, neighbour(): return lax.ppermute(value, 'exp', pairs)  97 us
    ppermute x54, starting transfers between devices, neighbour(): return lax.ppermute(value, 'exp', pairs)  64.6 us
    pallas_call x4, Pallas kernels, expert_mix(): pl.pallas_call(expert_kernel, grid=(count * EXPERT_CUTS,), in_specs=[rows...  43.5 us
    pallas_call x1, Pallas kernels, delta_local(): pl.pallas_call(lambda *refs: delta_kernel(blocks, *refs), grid_spec=pltpu...  31.7 us
    all_gather x1, waiting for transfers between devices, local(): w_piece = lax.all_gather(w_piece, 'exp', axis=0, tiled=True)  23.8 us
    all_to_all x1, waiting for transfers between devices, local(): lax.all_to_all(gated.reshape(owners, tok_dev, -1), 'exp', split_axis=0, c...  17.4 us
    dot_general x8, matrix products, mix(): jnp.dot(rows, w_half[i], preferred_element_type=F32)  16.9 us
    ppermute x6, waiting for transfers between devices, along_seq(): return lax.ppermute(value, 'seq', pairs)  8.42 us
  transfers between devices with their start and end apart: 63, of which 29 were waited for; matrix products, arithmetic and copies ran while one was open for 8% of the time, Pallas kernels for 22%

profile of v1, /device:TPU:32, one launch (start us, length us, event | category | flops | bytes accessed | tf_op | source)
XLA Modules:
  0.0 366.9 jit_solution(11186962216715095118)
XLA Ops:
  12.6 2.9 collective-permute-start.4
  15.5 3.0 collective-permute-start.1
  20.4 2.6 collective-permute-start
  23.1 4.7 %collective-permute-done.4 = bf16[64,2048]{1,0:T(8,128)(2,1)S(1)} collective-permute-done((bf16[64,2048]{1,0:T(8,128)(2,1)S(1)}, bf16[64,2048]{1,0:T(8,128)(2,1)S(1)}, u32[]{:S(2)}, u32[]{:S(2)}) %collective-permute-start.4) | collective-permute-done | bytes 262176 | tf_op jit(solution)/shard_map/ppermute | solution.py:350
  27.9 3.7 %collective-permute-done.2 = bf16[64,2048]{1,0:T(8,128)(2,1)S(1)} collective-permute-done((bf16[64,2048]{1,0:T(8,128)(2,1)S(1)}, bf16[64,2048]{1,0:T(8,128)(2,1)S(1)}, u32[]{:S(2)}, u32[]{:S(2)}) %collective-permute-start.2) | collective-permute-done | bytes 262176 | tf_op jit(solution)/shard_map/ppermute | solution.py:350
  33.4 23.8 %all-gather.4.cloned.1.call-done = bf16[4096,256]{1,0:T(8,128)(2,1)} async-done(((bf16[256,256]{1,0:T(8,128)(2,1)}), bf16[4096,256]{1,0:T(8,128)(2,1)}) %all-gather.4.cloned.1.call-update) | async-done | bytes 2097168 | tf_op jit(solution)/shard_map/all_gather | solution.py:474
  57.2 2.4 collective-permute-start.7
  59.9 3.0 collective-permute-start.13
  63.7 6.5 %collective-permute-done.7.refs_4_ = bf16[2,64,2048]{2,1,0:T(8,128)(2,1)} collective-permute-done((bf16[2,64,2048]{2,1,0:T(8,128)(2,1)S(1)}, bf16[2,64,2048]{2,1,0:T(8,128)(2,1)}, u32[]{:S(2)}, u32[]{:S(2)}) %collective-permute-start.7) | collective-permute-done | bytes 524320 | tf_op jit(solution)/shard_map/ppermute | solution.py:350
  70.2 2.4 collective-permute-start.12
  75.8 3.4 collective-permute-done.8.refs_7_
  79.3 8.3 %collective-permute-done.11.refs_8_ = bf16[2,64,2048]{2,1,0:T(8,128)(2,1)S(1)} collective-permute-done((bf16[2,64,2048]{2,1,0:T(8,128)(2,1)S(1)}, bf16[2,64,2048]{2,1,0:T(8,128)(2,1)S(1)}, u32[]{:S(2)}, u32[]{:S(2)}) %collective-permute-start.11) | collective-permute-done | bytes 524320 | tf_op jit(solution)/shard_map/ppermute | solution.py:350
  87.5 3.2 collective-permute-start.16
  94.5 2.5 collective-permute-done.10.refs_6_
  97.0 3.0 collective-permute-done.15.refs_13_
  100.0 4.1 %collective-permute-done.9.refs_5_ = bf16[2,64,2048]{2,1,0:T(8,128)(2,1)} collective-permute-done((bf16[2,64,2048]{2,1,0:T(8,128)(2,1)}, bf16[2,64,2048]{2,1,0:T(8,128)(2,1)}, u32[]{:S(2)}, u32[]{:S(2)}) %collective-permute-start.9) | collective-permute-done | bytes 524320 | tf_op jit(solution)/shard_map/ppermute | solution.py:350
  104.1 31.7 %delta_local.1 = (f32[2048,256]{1,0:T(8,128)}, f32[2048,256]{1,0:T(8,128)}, f32[2048,256]{1,0:T(8,128)}, f32[2,128,256]{2,1,0:T(8,128)}) custom-call(s32[3]{0:T(128)} %pad_add_fusion.refs_0_.place_ref, bf16[2,64,2048]{2,1,0:T(8,128)(2,1)} %pad_maximum_fusion.refs_1_, bf16[2,64,2048]{2,1,0:T(8,128)(2,1)} %copy-done.13, ...), custom_call_target="tpu_custom_call" | custom-call | flops 30000001024 | bytes 20000000 | tf_op jit(solution)/shard_map/delta_local/pallas_call | solution.py:184
  140.2 4.9 %collective-permute-start.20 = (bf16[2,128,256]{2,1,0:T(8,128)(2,1)S(1)}, bf16[2,128,256]{2,1,0:T(8,128)(2,1)S(1)}, u32[]{:S(2)}, u32[]{:S(2)}) collective-permute-start(bf16[2,128,256]{2,1,0:T(8,128)(2,1)S(1)} %pad_maximum_fusion.11), channel_id=1, source_target_pairs={{0,64},{16,80},{32,96},{48,112},{1,65},{17,81},{33,97},{49,113},{2... | collective-permute-start | bytes 393224 | tf_op jit(solution)/shard_map/ppermute | solution.py:418
  148.2 4.4 %collective-permute-done.21 = bf16[2,128,256]{2,1,0:T(8,128)(2,1)S(1)} collective-permute-done((bf16[2,128,256]{2,1,0:T(8,128)(2,1)S(1)}, bf16[2,128,256]{2,1,0:T(8,128)(2,1)S(1)}, u32[]{:S(2)}, u32[]{:S(2)}) %collective-permute-start.21) | collective-permute-done | bytes 131104 | tf_op jit(solution)/shard_map/ppermute | solution.py:418
  153.4 6.8 %delta_gate.1 = bf16[2048,256]{1,0:T(8,128)(2,1)} custom-call(s32[3]{0:T(128)} %pad_add_fusion.refs_0_.place_ref, bf16[4,2,128,256]{3,2,1,0:T(8,128)(2,1)} %pad_maximum_fusion.4.maps_ref, f32[2048,256]{1,0:T(8,128)} %get-tuple-element.68.base_ref, f32[2048,256]{1,0:T(8,128)} %get-tuple-element.69.reach_ref, f32[2048,256]{1,0:T(8,128)} %get-tuple-element.70.gate_ref, ...), custom_call_target="tpu_custom_call" | custom-call | flops 1000000000 | bytes 10000000 | tf_op jit(solution)/shard_map/delta_gate/pallas_call | solution.py:246
  160.3 2.3 copy.40
  162.6 4.4 %all-to-all-start = ((bf16[16,128,256]{1,2,0:T(8,128)(2,1)}), bf16[16,128,256]{1,2,0:T(8,128)(2,1)}, u32[]{:S(2)}, u32[]{:S(2)}) async-start(bf16[16,128,256]{1,2,0:T(8,128)(2,1)} %copy.40), calls=%async_computation | async-start | bytes 2097152 | tf_op jit(solution)/shard_map/all_to_all | solution.py:486
  167.0 17.4 %all-to-all-done = bf16[16,128,256]{1,2,0:T(8,128)(2,1)} async-done(((bf16[16,128,256]{1,2,0:T(8,128)(2,1)}), bf16[16,128,256]{1,2,0:T(8,128)(2,1)}, u32[]{:S(2)}, u32[]{:S(2)}) %all-to-all-start) | async-done | bytes 1048608 | tf_op jit(solution)/shard_map/all_to_all | solution.py:486
  187.5 2.6 fusion.17
  190.1 3.0 fusion.20
  193.1 2.5 fusion.23
  207.8 2.8 collective-permute-start.27
  213.8 3.6 convolution_multiply_fusion
  217.6 2.1 collective-permute-start.24
  219.7 2.9 collective-permute-done.29
  230.5 8.1 %collective-permute-done.33.refs_3_ = bf16[2,64,2048]{2,1,0:T(8,128)(2,1)S(1)} collective-permute-done((bf16[2,64,2048]{2,1,0:T(8,128)(2,1)S(1)}, bf16[2,64,2048]{2,1,0:T(8,128)(2,1)S(1)}, u32[]{:S(2)}, u32[]{:S(2)}) %collective-permute-start.33) | collective-permute-done | bytes 524320 | tf_op jit(solution)/shard_map/ppermute | solution.py:350
  238.8 10.9 %expert_mix.4 = (bf16[2,64,2048]{2,1,0:T(8,128)(2,1)S(1)}, bf16[2,64,2048]{2,1,0:T(8,128)(2,1)S(1)}, bf16[2,64,2048]{2,1,0:T(8,128)(2,1)S(1)}, bf16[2,64,2048]{2,1,0:T(8,128)(2,1)S(1)}) custom-call(bf16[2,64,2048]{2,1,0:T(8,128)(2,1)S(1)} %pad_maximum_fusion.6.refs_0_, bf16[2,64,2048]{2,1,0:T(8,128)(2,1)S(1)} %pad_maximum_fusion.7.refs_1_, ...), custom_call_target="tpu_custom_call" | custom-call | flops 6442450944 | bytes 16777216 | tf_op jit(solution)/shard_map/expert_mix/pallas_call | solution.py:321
  249.8 2.9 collective-permute-done.30.refs_0_
  256.8 10.9 %expert_mix.5 = (bf16[2,64,2048]{2,1,0:T(8,128)(2,1)S(1)}, bf16[2,64,2048]{2,1,0:T(8,128)(2,1)S(1)}, bf16[2,64,2048]{2,1,0:T(8,128)(2,1)S(1)}, bf16[2,64,2048]{2,1,0:T(8,128)(2,1)S(1)}) custom-call(bf16[2,64,2048]{2,1,0:T(8,128)(2,1)S(1)} %collective-permute-done.30.refs_0_, bf16[2,64,2048]{2,1,0:T(8,128)(2,1)S(1)} %collective-permute-done.31.refs_1_, ...), custom_call_target="tpu_custom_call" | custom-call | flops 6442450944 | bytes 16777216 | tf_op jit(solution)/shard_map/expert_mix/pallas_call | solution.py:321
  267.8 6.6 %collective-permute-done.38.refs_2_ = bf16[2,64,2048]{2,1,0:T(8,128)(2,1)S(1)} collective-permute-done((bf16[2,64,2048]{2,1,0:T(8,128)(2,1)S(1)}, bf16[2,64,2048]{2,1,0:T(8,128)(2,1)S(1)}, u32[]{:S(2)}, u32[]{:S(2)}) %collective-permute-start.38) | collective-permute-done | bytes 524320 | tf_op jit(solution)/shard_map/ppermute | solution.py:350
  274.3 10.9 %expert_mix.6 = (bf16[2,64,2048]{2,1,0:T(8,128)(2,1)S(1)}, bf16[2,64,2048]{2,1,0:T(8,128)(2,1)S(1)}, bf16[2,64,2048]{2,1,0:T(8,128)(2,1)S(1)}, bf16[2,64,2048]{2,1,0:T(8,128)(2,1)S(1)}) custom-call(bf16[2,64,2048]{2,1,0:T(8,128)(2,1)S(1)} %collective-permute-done.35.refs_0_, bf16[2,64,2048]{2,1,0:T(8,128)(2,1)S(1)} %collective-permute-done.36.refs_1_, ...), custom_call_target="tpu_custom_call" | custom-call | flops 6442450944 | bytes 16777216 | tf_op jit(solution)/shard_map/expert_mix/pallas_call | solution.py:321
  285.7 2.9 collective-permute-start.43
  288.5 3.5 collective-permute-start.45
  292.0 10.9 %expert_mix.7 = (bf16[2,64,2048]{2,1,0:T(8,128)(2,1)S(1)}, bf16[2,64,2048]{2,1,0:T(8,128)(2,1)S(1)}, bf16[2,64,2048]{2,1,0:T(8,128)(2,1)S(1)}, bf16[2,64,2048]{2,1,0:T(8,128)(2,1)S(1)}) custom-call(bf16[2,64,2048]{2,1,0:T(8,128)(2,1)S(1)} %collective-permute-done.34.refs_0_, bf16[2,64,2048]{2,1,0:T(8,128)(2,1)S(1)} %collective-permute-done.40.refs_1_, ...), custom_call_target="tpu_custom_call" | custom-call | flops 6442450944 | bytes 16777216 | tf_op jit(solution)/shard_map/expert_mix/pallas_call | solution.py:321
  305.0 3.2 collective-permute-start.54
  308.9 6.1 %collective-permute-done.47 = bf16[2,64,2048]{2,1,0:T(8,128)(2,1)S(1)} collective-permute-done((bf16[2,64,2048]{2,1,0:T(8,128)(2,1)S(1)}, bf16[2,64,2048]{2,1,0:T(8,128)(2,1)S(1)}, u32[]{:S(2)}, u32[]{:S(2)}) %collective-permute-start.47) | collective-permute-done | bytes 524320 | tf_op jit(solution)/shard_map/ppermute | solution.py:350
  316.7 9.8 %collective-permute-done.46 = bf16[2,64,2048]{2,1,0:T(8,128)(2,1)S(1)} collective-permute-done((bf16[2,64,2048]{2,1,0:T(8,128)(2,1)S(1)}, bf16[2,64,2048]{2,1,0:T(8,128)(2,1)S(1)}, u32[]{:S(2)}, u32[]{:S(2)}) %collective-permute-start.46) | collective-permute-done | bytes 524320 | tf_op jit(solution)/shard_map/ppermute | solution.py:350
  329.0 9.3 %collective-permute-done.57 = bf16[2,64,2048]{2,1,0:T(8,128)(2,1)S(1)} collective-permute-done((bf16[2,64,2048]{2,1,0:T(8,128)(2,1)S(1)}, bf16[2,64,2048]{2,1,0:T(8,128)(2,1)S(1)}, u32[]{:S(2)}, u32[]{:S(2)}) %collective-permute-start.57) | collective-permute-done | bytes 524320 | tf_op jit(solution)/shard_map/ppermute | solution.py:350
  340.5 3.8 %collective-permute-done.53 = bf16[2,64,2048]{2,1,0:T(8,128)(2,1)S(1)} collective-permute-done((bf16[2,64,2048]{2,1,0:T(8,128)(2,1)S(1)}, bf16[2,64,2048]{2,1,0:T(8,128)(2,1)S(1)}, u32[]{:S(2)}, u32[]{:S(2)}) %collective-permute-start.53) | collective-permute-done | bytes 524320 | tf_op jit(solution)/shard_map/ppermute | solution.py:350
  344.8 3.3 collective-permute-start.58
  350.3 1.9 collective-permute-done.55
  352.2 2.5 collective-permute-done.58
  354.7 3.1 collective-permute-done.59
  (200 shorter events, 70.7 us)
Async XLA Ops:
  6.5 50.6 %all-gather.4.cloned.1.call-start = ((), (), s32[]{:S(2)}) async-start(), calls=%async_computation.1 | async-start | bytes 2228224 | tf_op jit(solution)/shard_map/all_gather | solution.py:474
  8.3 179.2 %all-gather.6.cloned.1.call-start = ((), (), s32[]{:S(2)}) async-start(), calls=%async_computation.2 | async-start | bytes 10485760 | tf_op jit(solution)/shard_map/all_gather | solution.py:477
  12.6 15.2 %collective-permute-start.4 = (bf16[64,2048]{1,0:T(8,128)(2,1)S(1)}, bf16[64,2048]{1,0:T(8,128)(2,1)S(1)}, u32[]{:S(2)}, u32[]{:S(2)}) collective-permute-start(bf16[64,2048]{1,0:T(8,128)(2,1)S(1)} %get-tuple-element.143), channel_id=1, source_target_pairs={{0,8},{1,9},{2,10},{3,11},{4,12},{5,13},{6,14},{7,15},{8,0},{9,1},... | collective-permute-start | bytes 786440 | tf_op jit(solution)/shard_map/ppermute | solution.py:350
  15.5 12.4 %collective-permute-start.1 = (bf16[64,2048]{1,0:T(8,128)(2,1)S(1)}, bf16[64,2048]{1,0:T(8,128)(2,1)S(1)}, u32[]{:S(2)}, u32[]{:S(2)}) collective-permute-start(bf16[64,2048]{1,0:T(8,128)(2,1)S(1)} %get-tuple-element.144), channel_id=1, source_target_pairs={{0,2},{1,3},{2,0},{3,1},{4,6},{5,7},{6,4},{7,5},{8,10},{9,11},{10,... | collective-permute-start | bytes 786440 | tf_op jit(solution)/shard_map/ppermute | solution.py:350
  18.5 13.1 %collective-permute-start.2 = (bf16[64,2048]{1,0:T(8,128)(2,1)S(1)}, bf16[64,2048]{1,0:T(8,128)(2,1)S(1)}, u32[]{:S(2)}, u32[]{:S(2)}) collective-permute-start(bf16[64,2048]{1,0:T(8,128)(2,1)S(1)} %get-tuple-element.144), channel_id=1, source_target_pairs={{0,1},{1,2},{2,3},{3,0},{4,5},{5,6},{6,7},{7,4},{8,9},{9,10},{10,1... | collective-permute-start | bytes 786440 | tf_op jit(solution)/shard_map/ppermute | solution.py:350
  19.1 12.5 %collective-permute-start.3 = (bf16[64,2048]{1,0:T(8,128)(2,1)S(1)}, bf16[64,2048]{1,0:T(8,128)(2,1)S(1)}, u32[]{:S(2)}, u32[]{:S(2)}) collective-permute-start(bf16[64,2048]{1,0:T(8,128)(2,1)S(1)} %get-tuple-element.143), channel_id=1, source_target_pairs={{0,12},{1,13},{2,14},{3,15},{4,0},{5,1},{6,2},{7,3},{8,4},{9,5},{1... | collective-permute-start | bytes 786440 | tf_op jit(solution)/shard_map/ppermute | solution.py:350
  20.4 12.1 %collective-permute-start = (bf16[64,2048]{1,0:T(8,128)(2,1)S(1)}, bf16[64,2048]{1,0:T(8,128)(2,1)S(1)}, u32[]{:S(2)}, u32[]{:S(2)}) collective-permute-start(bf16[64,2048]{1,0:T(8,128)(2,1)S(1)} %get-tuple-element.144), channel_id=1, source_target_pairs={{0,3},{1,0},{2,1},{3,2},{4,7},{5,4},{6,5},{7,6},{8,11},{9,8},{10,9... | collective-permute-start | bytes 786440 | tf_op jit(solution)/shard_map/ppermute | solution.py:350
  57.2 13.0 %collective-permute-start.7 = (bf16[2,64,2048]{2,1,0:T(8,128)(2,1)S(1)}, bf16[2,64,2048]{2,1,0:T(8,128)(2,1)}, u32[]{:S(2)}, u32[]{:S(2)}) collective-permute-start(bf16[2,64,2048]{2,1,0:T(8,128)(2,1)S(1)} %pad_maximum_fusion.1.refs_2_), channel_id=1, source_target_pairs={{0,12},{1,13},{2,14},{3,15},{4,0},{5,1},{6,2},{7,3},{8,4},{9,5},{1... | collective-permute-start | bytes 1572872 | tf_op jit(solution)/shard_map/ppermute | solution.py:350
  59.6 14.1 %collective-permute-start.14 = (bf16[2,64,2048]{2,1,0:T(8,128)(2,1)}, bf16[2,64,2048]{2,1,0:T(8,128)(2,1)}, u32[]{:S(2)}, u32[]{:S(2)}) collective-permute-start(bf16[2,64,2048]{2,1,0:T(8,128)(2,1)} %pad_maximum_fusion.2.refs_9_), channel_id=1, source_target_pairs={{0,1},{1,2},{2,3},{3,0},{4,5},{5,6},{6,7},{7,4},{8,9},{9,10},{10,1... | collective-permute-start | bytes 1572872 | tf_op jit(solution)/shard_map/ppermute | solution.py:350
  59.9 14.4 %collective-permute-start.13 = (bf16[2,64,2048]{2,1,0:T(8,128)(2,1)S(1)}, bf16[2,64,2048]{2,1,0:T(8,128)(2,1)}, u32[]{:S(2)}, u32[]{:S(2)}) collective-permute-start(bf16[2,64,2048]{2,1,0:T(8,128)(2,1)S(1)} %pad_maximum_fusion.3.refs_10_), channel_id=1, source_target_pairs={{0,3},{1,0},{2,1},{3,2},{4,7},{5,4},{6,5},{7,6},{8,11},{9,8},{10,9... | collective-permute-start | bytes 1572872 | tf_op jit(solution)/shard_map/ppermute | solution.py:350
  62.9 16.4 %collective-permute-start.8 = (bf16[2,64,2048]{2,1,0:T(8,128)(2,1)}, bf16[2,64,2048]{2,1,0:T(8,128)(2,1)}, u32[]{:S(2)}, u32[]{:S(2)}) collective-permute-start(bf16[2,64,2048]{2,1,0:T(8,128)(2,1)} %pad_maximum_fusion.refs_1_), channel_id=1, source_target_pairs={{0,4},{1,5},{2,6},{3,7},{4,8},{5,9},{6,10},{7,11},{8,12},{9,13},{1... | collective-permute-start | bytes 1572872 | tf_op jit(solution)/shard_map/ppermute | solution.py:350
  62.9 24.6 %collective-permute-start.11 = (bf16[2,64,2048]{2,1,0:T(8,128)(2,1)S(1)}, bf16[2,64,2048]{2,1,0:T(8,128)(2,1)S(1)}, u32[]{:S(2)}, u32[]{:S(2)}) collective-permute-start(bf16[2,64,2048]{2,1,0:T(8,128)(2,1)S(1)} %pad_maximum_fusion.1.refs_2_), channel_id=1, source_target_pairs={{0,4},{1,5},{2,6},{3,7},{4,8},{5,9},{6,10},{7,11},{8,12},{9,13},{1... | collective-permute-start | bytes 1572872 | tf_op jit(solution)/shard_map/ppermute | solution.py:350
  70.2 17.3 %collective-permute-start.12 = (bf16[2,64,2048]{2,1,0:T(8,128)(2,1)}, bf16[2,64,2048]{2,1,0:T(8,128)(2,1)S(1)}, u32[]{:S(2)}, u32[]{:S(2)}) collective-permute-start(bf16[2,64,2048]{2,1,0:T(8,128)(2,1)} %pad_maximum_fusion.2.refs_9_), channel_id=1, source_target_pairs={{0,3},{1,0},{2,1},{3,2},{4,7},{5,4},{6,5},{7,6},{8,11},{9,8},{10,9... | collective-permute-start | bytes 1572872 | tf_op jit(solution)/shard_map/ppermute | solution.py:350
  73.7 17.1 %collective-permute-start.17 = (bf16[2,64,2048]{2,1,0:T(8,128)(2,1)S(1)}, bf16[2,64,2048]{2,1,0:T(8,128)(2,1)S(1)}, u32[]{:S(2)}, u32[]{:S(2)}) collective-permute-start(bf16[2,64,2048]{2,1,0:T(8,128)(2,1)S(1)} %pad_maximum_fusion.3.refs_10_), channel_id=1, source_target_pairs={{0,1},{1,2},{2,3},{3,0},{4,5},{5,6},{6,7},{7,4},{8,9},{9,10},{10,1... | collective-permute-start | bytes 1572872 | tf_op jit(solution)/shard_map/ppermute | solution.py:350
  74.3 20.2 %collective-permute-start.6 = (bf16[2,64,2048]{2,1,0:T(8,128)(2,1)}, bf16[2,64,2048]{2,1,0:T(8,128)(2,1)}, u32[]{:S(2)}, u32[]{:S(2)}) collective-permute-start(bf16[2,64,2048]{2,1,0:T(8,128)(2,1)} %pad_maximum_fusion.refs_1_), channel_id=1, source_target_pairs={{0,12},{1,13},{2,14},{3,15},{4,0},{5,1},{6,2},{7,3},{8,4},{9,5},{1... | collective-permute-start | bytes 1572872 | tf_op jit(solution)/shard_map/ppermute | solution.py:350
  79.2 17.7 %collective-permute-start.10 = (bf16[2,64,2048]{2,1,0:T(8,128)(2,1)}, bf16[2,64,2048]{2,1,0:T(8,128)(2,1)}, u32[]{:S(2)}, u32[]{:S(2)}) collective-permute-start(bf16[2,64,2048]{2,1,0:T(8,128)(2,1)} %collective-permute-done.7.refs_4_), channel_id=1, source_target_pairs={{0,12},{1,13},{2,14},{3,15},{4,0},{5,1},{6,2},{7,3},{8,4},{9,5},{1... | collective-permute-start | bytes 1572872 | tf_op jit(solution)/shard_map/ppermute | solution.py:350
  87.5 12.5 %collective-permute-start.15 = (bf16[2,64,2048]{2,1,0:T(8,128)(2,1)}, bf16[2,64,2048]{2,1,0:T(8,128)(2,1)S(1)}, u32[]{:S(2)}, u32[]{:S(2)}) collective-permute-start(bf16[2,64,2048]{2,1,0:T(8,128)(2,1)} %collective-permute-done.14.refs_15_), channel_id=1, source_target_pairs={{0,1},{1,2},{2,3},{3,0},{4,5},{5,6},{6,7},{7,4},{8,9},{9,10},{10,1... | collective-permute-start | bytes 1572872 | tf_op jit(solution)/shard_map/ppermute | solution.py:350
  87.5 12.5 %collective-permute-start.16 = (bf16[2,64,2048]{2,1,0:T(8,128)(2,1)}, bf16[2,64,2048]{2,1,0:T(8,128)(2,1)}, u32[]{:S(2)}, u32[]{:S(2)}) collective-permute-start(bf16[2,64,2048]{2,1,0:T(8,128)(2,1)} %collective-permute-done.13.refs_12_), channel_id=1, source_target_pairs={{0,3},{1,0},{2,1},{3,2},{4,7},{5,4},{6,5},{7,6},{8,11},{9,8},{10,9... | collective-permute-start | bytes 1572872 | tf_op jit(solution)/shard_map/ppermute | solution.py:350
  91.6 12.5 %collective-permute-start.9 = (bf16[2,64,2048]{2,1,0:T(8,128)(2,1)}, bf16[2,64,2048]{2,1,0:T(8,128)(2,1)}, u32[]{:S(2)}, u32[]{:S(2)}) collective-permute-start(bf16[2,64,2048]{2,1,0:T(8,128)(2,1)} %collective-permute-done.8.refs_7_), channel_id=1, source_target_pairs={{0,4},{1,5},{2,6},{3,7},{4,8},{5,9},{6,10},{7,11},{8,12},{9,13},{1... | collective-permute-start | bytes 1572872 | tf_op jit(solution)/shard_map/ppermute | solution.py:350
  162.6 21.7 %all-to-all-start = ((bf16[16,128,256]{1,2,0:T(8,128)(2,1)}), bf16[16,128,256]{1,2,0:T(8,128)(2,1)}, u32[]{:S(2)}, u32[]{:S(2)}) async-start(bf16[16,128,256]{1,2,0:T(8,128)(2,1)} %copy.40), calls=%async_computation | async-start | bytes 2097152 | tf_op jit(solution)/shard_map/all_to_all | solution.py:486
  207.4 15.2 %collective-permute-start.29 = (bf16[64,2048]{1,0:T(8,128)(2,1)}, bf16[64,2048]{1,0:T(8,128)(2,1)}, u32[]{:S(2)}, u32[]{:S(2)}) collective-permute-start(bf16[64,2048]{1,0:T(8,128)(2,1)} %get-tuple-element.139), channel_id=1, source_target_pairs={{0,4},{1,5},{2,6},{3,7},{4,8},{5,9},{6,10},{7,11},{8,12},{9,13},{1... | collective-permute-start | bytes 786440 | tf_op jit(solution)/shard_map/ppermute | solution.py:350
  207.8 16.0 %collective-permute-start.27 = (bf16[64,2048]{1,0:T(8,128)(2,1)}, bf16[64,2048]{1,0:T(8,128)(2,1)}, u32[]{:S(2)}, u32[]{:S(2)}) collective-permute-start(bf16[64,2048]{1,0:T(8,128)(2,1)} %get-tuple-element.139), channel_id=1, source_target_pairs={{0,12},{1,13},{2,14},{3,15},{4,0},{5,1},{6,2},{7,3},{8,4},{9,5},{1... | collective-permute-start | bytes 786440 | tf_op jit(solution)/shard_map/ppermute | solution.py:350
  210.7 15.1 %collective-permute-start.25 = (bf16[64,2048]{1,0:T(8,128)(2,1)}, bf16[64,2048]{1,0:T(8,128)(2,1)}, u32[]{:S(2)}, u32[]{:S(2)}) collective-permute-start(bf16[64,2048]{1,0:T(8,128)(2,1)} %get-tuple-element.140), channel_id=1, source_target_pairs={{0,2},{1,3},{2,0},{3,1},{4,6},{5,7},{6,4},{7,5},{8,10},{9,11},{10,... | collective-permute-start | bytes 786440 | tf_op jit(solution)/shard_map/ppermute | solution.py:350
  211.5 15.5 %collective-permute-start.26 = (bf16[64,2048]{1,0:T(8,128)(2,1)}, bf16[64,2048]{1,0:T(8,128)(2,1)}, u32[]{:S(2)}, u32[]{:S(2)}) collective-permute-start(bf16[64,2048]{1,0:T(8,128)(2,1)} %get-tuple-element.140), channel_id=1, source_target_pairs={{0,1},{1,2},{2,3},{3,0},{4,5},{5,6},{6,7},{7,4},{8,9},{9,10},{10,1... | collective-permute-start | bytes 786440 | tf_op jit(solution)/shard_map/ppermute | solution.py:350
  223.7 14.9 %collective-permute-start.33 = (bf16[2,64,2048]{2,1,0:T(8,128)(2,1)S(1)}, bf16[2,64,2048]{2,1,0:T(8,128)(2,1)S(1)}, u32[]{:S(2)}, u32[]{:S(2)}) collective-permute-start(bf16[2,64,2048]{2,1,0:T(8,128)(2,1)S(1)} %pad_maximum_fusion.9.refs_3_), channel_id=1, source_target_pairs={{0,3},{1,0},{2,1},{3,2},{4,7},{5,4},{6,5},{7,6},{8,11},{9,8},{10,9... | collective-permute-start | bytes 1572872 | tf_op jit(solution)/shard_map/ppermute | solution.py:350
  224.9 24.8 %collective-permute-start.32 = (bf16[2,64,2048]{2,1,0:T(8,128)(2,1)S(1)}, bf16[2,64,2048]{2,1,0:T(8,128)(2,1)S(1)}, u32[]{:S(2)}, u32[]{:S(2)}) collective-permute-start(bf16[2,64,2048]{2,1,0:T(8,128)(2,1)S(1)} %pad_maximum_fusion.8.refs_2_), channel_id=1, source_target_pairs={{0,3},{1,0},{2,1},{3,2},{4,7},{5,4},{6,5},{7,6},{8,11},{9,8},{10,9... | collective-permute-start | bytes 1572872 | tf_op jit(solution)/shard_map/ppermute | solution.py:350
  225.8 30.4 %collective-permute-start.37 = (bf16[2,64,2048]{2,1,0:T(8,128)(2,1)S(1)}, bf16[2,64,2048]{2,1,0:T(8,128)(2,1)S(1)}, u32[]{:S(2)}, u32[]{:S(2)}) collective-permute-start(bf16[2,64,2048]{2,1,0:T(8,128)(2,1)S(1)} %pad_maximum_fusion.8.refs_2_), channel_id=1, source_target_pairs={{0,1},{1,2},{2,3},{3,0},{4,5},{5,6},{6,7},{7,4},{8,9},{9,10},{10,1... | collective-permute-start | bytes 1572872 | tf_op jit(solution)/shard_map/ppermute | solution.py:350
  228.1 21.7 %collective-permute-start.31 = (bf16[2,64,2048]{2,1,0:T(8,128)(2,1)S(1)}, bf16[2,64,2048]{2,1,0:T(8,128)(2,1)S(1)}, u32[]{:S(2)}, u32[]{:S(2)}) collective-permute-start(bf16[2,64,2048]{2,1,0:T(8,128)(2,1)S(1)} %pad_maximum_fusion.7.refs_1_), channel_id=1, source_target_pairs={{0,12},{1,13},{2,14},{3,15},{4,0},{5,1},{6,2},{7,3},{8,4},{9,5},{1... | collective-permute-start | bytes 1572872 | tf_op jit(solution)/shard_map/ppermute | solution.py:350
  228.9 23.9 %collective-permute-start.30 = (bf16[2,64,2048]{2,1,0:T(8,128)(2,1)S(1)}, bf16[2,64,2048]{2,1,0:T(8,128)(2,1)S(1)}, u32[]{:S(2)}, u32[]{:S(2)}) collective-permute-start(bf16[2,64,2048]{2,1,0:T(8,128)(2,1)S(1)} %pad_maximum_fusion.6.refs_0_), channel_id=1, source_target_pairs={{0,12},{1,13},{2,14},{3,15},{4,0},{5,1},{6,2},{7,3},{8,4},{9,5},{1... | collective-permute-start | bytes 1572872 | tf_op jit(solution)/shard_map/ppermute | solution.py:350
  238.6 17.7 %collective-permute-start.34 = (bf16[2,64,2048]{2,1,0:T(8,128)(2,1)S(1)}, bf16[2,64,2048]{2,1,0:T(8,128)(2,1)S(1)}, u32[]{:S(2)}, u32[]{:S(2)}) collective-permute-start(bf16[2,64,2048]{2,1,0:T(8,128)(2,1)S(1)} %pad_maximum_fusion.6.refs_0_), channel_id=1, source_target_pairs={{0,4},{1,5},{2,6},{3,7},{4,8},{5,9},{6,10},{7,11},{8,12},{9,13},{1... | collective-permute-start | bytes 1572872 | tf_op jit(solution)/shard_map/ppermute | solution.py:350
  249.7 35.5 %collective-permute-start.41 = (bf16[2,64,2048]{2,1,0:T(8,128)(2,1)S(1)}, bf16[2,64,2048]{2,1,0:T(8,128)(2,1)S(1)}, u32[]{:S(2)}, u32[]{:S(2)}) collective-permute-start(bf16[2,64,2048]{2,1,0:T(8,128)(2,1)S(1)} %pad_maximum_fusion.9.refs_3_), channel_id=1, source_target_pairs={{0,1},{1,2},{2,3},{3,0},{4,5},{5,6},{6,7},{7,4},{8,9},{9,10},{10,1... | collective-permute-start | bytes 1572872 | tf_op jit(solution)/shard_map/ppermute | solution.py:350
  252.7 14.9 %collective-permute-start.39 = (bf16[2,64,2048]{2,1,0:T(8,128)(2,1)S(1)}, bf16[2,64,2048]{2,1,0:T(8,128)(2,1)S(1)}, u32[]{:S(2)}, u32[]{:S(2)}) collective-permute-start(bf16[2,64,2048]{2,1,0:T(8,128)(2,1)S(1)} %collective-permute-done.33.refs_3_), channel_id=1, source_target_pairs={{0,3},{1,0},{2,1},{3,2},{4,7},{5,4},{6,5},{7,6},{8,11},{9,8},{10,9... | collective-permute-start | bytes 1572872 | tf_op jit(solution)/shard_map/ppermute | solution.py:350
  254.4 19.9 %collective-permute-start.36 = (bf16[2,64,2048]{2,1,0:T(8,128)(2,1)S(1)}, bf16[2,64,2048]{2,1,0:T(8,128)(2,1)S(1)}, u32[]{:S(2)}, u32[]{:S(2)}) collective-permute-start(bf16[2,64,2048]{2,1,0:T(8,128)(2,1)S(1)} %collective-permute-done.31.refs_1_), channel_id=1, source_target_pairs={{0,12},{1,13},{2,14},{3,15},{4,0},{5,1},{6,2},{7,3},{8,4},{9,5},{1... | collective-permute-start | bytes 1572872 | tf_op jit(solution)/shard_map/ppermute | solution.py:350
  256.2 18.1 %collective-permute-start.38 = (bf16[2,64,2048]{2,1,0:T(8,128)(2,1)S(1)}, bf16[2,64,2048]{2,1,0:T(8,128)(2,1)S(1)}, u32[]{:S(2)}, u32[]{:S(2)}) collective-permute-start(bf16[2,64,2048]{2,1,0:T(8,128)(2,1)S(1)} %collective-permute-done.37.refs_2_), channel_id=1, source_target_pairs={{0,1},{1,2},{2,3},{3,0},{4,5},{5,6},{6,7},{7,4},{8,9},{9,10},{10,1... | collective-permute-start | bytes 1572872 | tf_op jit(solution)/shard_map/ppermute | solution.py:350
  256.3 18.1 %collective-permute-start.35 = (bf16[2,64,2048]{2,1,0:T(8,128)(2,1)S(1)}, bf16[2,64,2048]{2,1,0:T(8,128)(2,1)S(1)}, u32[]{:S(2)}, u32[]{:S(2)}) collective-permute-start(bf16[2,64,2048]{2,1,0:T(8,128)(2,1)S(1)} %collective-permute-done.34.refs_0_), channel_id=1, source_target_pairs={{0,4},{1,5},{2,6},{3,7},{4,8},{5,9},{6,10},{7,11},{8,12},{9,13},{1... | collective-permute-start | bytes 1572872 | tf_op jit(solution)/shard_map/ppermute | solution.py:350
  267.7 17.6 %collective-permute-start.40 = (bf16[2,64,2048]{2,1,0:T(8,128)(2,1)S(1)}, bf16[2,64,2048]{2,1,0:T(8,128)(2,1)S(1)}, u32[]{:S(2)}, u32[]{:S(2)}) collective-permute-start(bf16[2,64,2048]{2,1,0:T(8,128)(2,1)S(1)} %pad_maximum_fusion.7.refs_1_), channel_id=1, source_target_pairs={{0,4},{1,5},{2,6},{3,7},{4,8},{5,9},{6,10},{7,11},{8,12},{9,13},{1... | collective-permute-start | bytes 1572872 | tf_op jit(solution)/shard_map/ppermute | solution.py:350
  285.2 19.4 %collective-permute-start.42 = (bf16[2,64,2048]{2,1,0:T(8,128)(2,1)S(1)}, bf16[2,64,2048]{2,1,0:T(8,128)(2,1)S(1)}, u32[]{:S(2)}, u32[]{:S(2)}) collective-permute-start(bf16[2,64,2048]{2,1,0:T(8,128)(2,1)S(1)} %get-tuple-element.99), channel_id=1, source_target_pairs={{0,4},{1,5},{2,6},{3,7},{4,8},{5,9},{6,10},{7,11},{8,12},{9,13},{1... | collective-permute-start | bytes 1572872 | tf_op jit(solution)/shard_map/ppermute | solution.py:350
  285.7 19.3 %collective-permute-start.43 = (bf16[2,64,2048]{2,1,0:T(8,128)(2,1)S(1)}, bf16[2,64,2048]{2,1,0:T(8,128)(2,1)S(1)}, u32[]{:S(2)}, u32[]{:S(2)}) collective-permute-start(bf16[2,64,2048]{2,1,0:T(8,128)(2,1)S(1)} %get-tuple-element.100), channel_id=1, source_target_pairs={{0,12},{1,13},{2,14},{3,15},{4,0},{5,1},{6,2},{7,3},{8,4},{9,5},{1... | collective-permute-start | bytes 1572872 | tf_op jit(solution)/shard_map/ppermute | solution.py:350
  288.5 16.4 %collective-permute-start.44 = (bf16[2,64,2048]{2,1,0:T(8,128)(2,1)S(1)}, bf16[2,64,2048]{2,1,0:T(8,128)(2,1)S(1)}, u32[]{:S(2)}, u32[]{:S(2)}) collective-permute-start(bf16[2,64,2048]{2,1,0:T(8,128)(2,1)S(1)} %get-tuple-element.101), channel_id=1, source_target_pairs={{0,1},{1,2},{2,3},{3,0},{4,5},{5,6},{6,7},{7,4},{8,9},{9,10},{10,1... | collective-permute-start | bytes 1572872 | tf_op jit(solution)/shard_map/ppermute | solution.py:350
  288.5 19.7 %collective-permute-start.45 = (bf16[2,64,2048]{2,1,0:T(8,128)(2,1)S(1)}, bf16[2,64,2048]{2,1,0:T(8,128)(2,1)S(1)}, u32[]{:S(2)}, u32[]{:S(2)}) collective-permute-start(bf16[2,64,2048]{2,1,0:T(8,128)(2,1)S(1)} %get-tuple-element.102), channel_id=1, source_target_pairs={{0,3},{1,0},{2,1},{3,2},{4,7},{5,4},{6,5},{7,6},{8,11},{9,8},{10,9... | collective-permute-start | bytes 1572872 | tf_op jit(solution)/shard_map/ppermute | solution.py:350
  302.9 12.2 %collective-permute-start.47 = (bf16[2,64,2048]{2,1,0:T(8,128)(2,1)S(1)}, bf16[2,64,2048]{2,1,0:T(8,128)(2,1)S(1)}, u32[]{:S(2)}, u32[]{:S(2)}) collective-permute-start(bf16[2,64,2048]{2,1,0:T(8,128)(2,1)S(1)} %get-tuple-element.108), channel_id=1, source_target_pairs={{0,12},{1,13},{2,14},{3,15},{4,0},{5,1},{6,2},{7,3},{8,4},{9,5},{1... | collective-permute-start | bytes 1572872 | tf_op jit(solution)/shard_map/ppermute | solution.py:350
  304.6 23.4 %collective-permute-start.49 = (bf16[2,64,2048]{2,1,0:T(8,128)(2,1)S(1)}, bf16[2,64,2048]{2,1,0:T(8,128)(2,1)S(1)}, u32[]{:S(2)}, u32[]{:S(2)}) collective-permute-start(bf16[2,64,2048]{2,1,0:T(8,128)(2,1)S(1)} %get-tuple-element.110), channel_id=1, source_target_pairs={{0,4},{1,5},{2,6},{3,7},{4,8},{5,9},{6,10},{7,11},{8,12},{9,13},{1... | collective-permute-start | bytes 1572872 | tf_op jit(solution)/shard_map/ppermute | solution.py:350
  305.0 23.9 %collective-permute-start.56 = (bf16[2,64,2048]{2,1,0:T(8,128)(2,1)S(1)}, bf16[2,64,2048]{2,1,0:T(8,128)(2,1)S(1)}, u32[]{:S(2)}, u32[]{:S(2)}) collective-permute-start(bf16[2,64,2048]{2,1,0:T(8,128)(2,1)S(1)} %get-tuple-element.118), channel_id=1, source_target_pairs={{0,1},{1,2},{2,3},{3,0},{4,5},{5,6},{6,7},{7,4},{8,9},{9,10},{10,1... | collective-permute-start | bytes 1572872 | tf_op jit(solution)/shard_map/ppermute | solution.py:350
  305.0 35.5 %collective-permute-start.54 = (bf16[2,64,2048]{2,1,0:T(8,128)(2,1)S(1)}, bf16[2,64,2048]{2,1,0:T(8,128)(2,1)S(1)}, u32[]{:S(2)}, u32[]{:S(2)}) collective-permute-start(bf16[2,64,2048]{2,1,0:T(8,128)(2,1)S(1)} %get-tuple-element.116), channel_id=1, source_target_pairs={{0,3},{1,0},{2,1},{3,2},{4,7},{5,4},{6,5},{7,6},{8,11},{9,8},{10,9... | collective-permute-start | bytes 1572872 | tf_op jit(solution)/shard_map/ppermute | solution.py:350
  308.4 18.2 %collective-permute-start.46 = (bf16[2,64,2048]{2,1,0:T(8,128)(2,1)S(1)}, bf16[2,64,2048]{2,1,0:T(8,128)(2,1)S(1)}, u32[]{:S(2)}, u32[]{:S(2)}) collective-permute-start(bf16[2,64,2048]{2,1,0:T(8,128)(2,1)S(1)} %add_convert_fusion.7), channel_id=1, source_target_pairs={{0,4},{1,5},{2,6},{3,7},{4,8},{5,9},{6,10},{7,11},{8,12},{9,13},{1... | collective-permute-start | bytes 1572872 | tf_op jit(solution)/shard_map/ppermute | solution.py:350
  315.0 14.0 %collective-permute-start.50 = (bf16[2,64,2048]{2,1,0:T(8,128)(2,1)S(1)}, bf16[2,64,2048]{2,1,0:T(8,128)(2,1)S(1)}, u32[]{:S(2)}, u32[]{:S(2)}) collective-permute-start(bf16[2,64,2048]{2,1,0:T(8,128)(2,1)S(1)} %add_convert_fusion.5), channel_id=1, source_target_pairs={{0,12},{1,13},{2,14},{3,15},{4,0},{5,1},{6,2},{7,3},{8,4},{9,5},{1... | collective-permute-start | bytes 1572872 | tf_op jit(solution)/shard_map/ppermute | solution.py:350
  328.0 16.3 %collective-permute-start.53 = (bf16[2,64,2048]{2,1,0:T(8,128)(2,1)S(1)}, bf16[2,64,2048]{2,1,0:T(8,128)(2,1)S(1)}, u32[]{:S(2)}, u32[]{:S(2)}) collective-permute-start(bf16[2,64,2048]{2,1,0:T(8,128)(2,1)S(1)} %add_convert_fusion.3), channel_id=1, source_target_pairs={{0,1},{1,2},{2,3},{3,0},{4,5},{5,6},{6,7},{7,4},{8,9},{9,10},{10,1... | collective-permute-start | bytes 1572872 | tf_op jit(solution)/shard_map/ppermute | solution.py:350
  328.9 21.0 %collective-permute-start.48 = (bf16[64,2048]{1,0:T(8,128)(2,1)S(1)}, bf16[64,2048]{1,0:T(8,128)(2,1)S(1)}, u32[]{:S(2)}, u32[]{:S(2)}) collective-permute-start(bf16[64,2048]{1,0:T(8,128)(2,1)S(1)} %slice_bitcast_fusion.8), channel_id=1, source_target_pairs={{0,1},{1,2},{2,3},{3,0},{4,5},{5,6},{6,7},{7,4},{8,9},{9,10},{10,1... | collective-permute-start | bytes 786440 | tf_op jit(solution)/shard_map/ppermute | solution.py:350
  (39 other events, 699.5 us)
Sparse Core Ops, SparseCore 0:
  9.5 47.6 all-gather.3
  58.8 82.5 all-gather.5

commit v2 on v0

--- a/solution.py
+++ b/solution.py
@@ -48,29 +48,27 @@
     return mm(jnp.concatenate([ah, al], axis=1), jnp.concatenate([bh, bh], axis=0)) + mm(ah, bl)
 
 
-def delta_kernel(
-    blocks,
-    place_ref,
-    *refs,
-):
-    gathered, refs = refs[: 2 * SIDE], refs[2 * SIDE :]
+def delta_kernel(blocks, spots, place_ref, *refs):
+    gathered, refs = refs[: len(spots)], refs[len(spots) :]
     query_ref, key_ref, value_ref, outgate_ref, cum_ref, rate_ref = refs[:6]
-    base_ref, reach_ref, gate_ref, total_ref, state, held, lines, proj_ref, arrived = refs[6:]
+    base_ref, reach_ref, gate_ref, total_ref, state, held, lines, proj_ref, pair_ref, arrived = refs[6:]
     step = pl.program_id(0)
 
     @pl.when(step == 0)
     def _():
         copies = [
-            pltpu.make_async_copy(ref, held.at[i // SIDE, i % SIDE], arrived.at[i])
-            for i, ref in enumerate(gathered)
+            pltpu.make_async_copy(ref, held.at[group, away, pl.ds(start, count)], arrived.at[i])
+            for i, (ref, (group, away, start, count)) in enumerate(zip(gathered, spots))
         ]
         for copy in copies:
             copy.start()
+        pair_ref[:, :DK] = query_ref[...]
+        pair_ref[:, DK:] = key_ref[...]
         for copy in copies:
             copy.wait()
 
     part = held.shape[3]
-    pair = 2
+    pair = 4
 
     def project(c, carry):
         for u in range(pair):
@@ -81,8 +79,7 @@
             lines[u * BLOCK + part : (u + 1) * BLOCK] = held[1, far_x, far_y]
         x = lines[...]
         span = pl.ds(pl.multiple_of(c * pair * BLOCK, pair * BLOCK), pair * BLOCK)
-        proj_ref[span, 0:DK] = mm(x, query_ref[...])
-        proj_ref[span, DK : 2 * DK] = mm(x, key_ref[...])
+        proj_ref[span, : 2 * DK] = mm(x, pair_ref[...])
         proj_ref[span, 2 * DK :] = mm(x, value_ref[...])
         gate_ref[span, :] = mm(x, outgate_ref[...])
         return carry
@@ -170,18 +167,27 @@
 
 
 def delta_local(place, firsts, seconds, weights, cumulative, rates):
-    side, part, width = firsts[0].shape
+    pieces, spots = [], []
+    for group, blocks in enumerate((firsts, seconds)):
+        for away, parts in enumerate(blocks):
+            start = 0
+            for piece in parts:
+                pieces.append(piece)
+                spots.append((group, away, start, piece.shape[0]))
+                start += piece.shape[0]
+    side = SIDE
+    _, part, width = pieces[0].shape
     tokens = 2 * side * side * part
     blocks = 8
     whole = lambda i, p: (0, 0)
     lines = pl.BlockSpec((blocks * BLOCK, 2 * DV), lambda i, p: (i, 0))
     rates_spec = pl.BlockSpec((2, blocks, BLOCK), lambda i, p: (0, i, 0))
     return pl.pallas_call(
-        lambda *refs: delta_kernel(blocks, *refs),
+        lambda *refs: delta_kernel(blocks, spots, *refs),
         grid_spec=pltpu.PrefetchScalarGridSpec(
             num_scalar_prefetch=1,
             grid=(tokens // (blocks * BLOCK),),
-            in_specs=[pl.BlockSpec(memory_space=pl.ANY)] * (2 * side)
+            in_specs=[pl.BlockSpec(memory_space=pl.ANY)] * len(pieces)
             + [pl.BlockSpec(w.shape, whole, pipeline_mode=pl.Buffered(1)) for w in weights]
             + [rates_spec, rates_spec],
             out_specs=[
@@ -193,9 +199,10 @@
             scratch_shapes=[
                 pltpu.VMEM((2, DK, DK + DV), F32),
                 pltpu.VMEM((2, side, side, part, width), BF16),
-                pltpu.VMEM((2 * BLOCK, width), BF16),
+                pltpu.VMEM((4 * BLOCK, width), BF16),
                 pltpu.VMEM((blocks * BLOCK, 2 * DK + 2 * DV), F32),
-                pltpu.SemaphoreType.DMA((2 * side,)),
+                pltpu.VMEM((width, 2 * DK), BF16),
+                pltpu.SemaphoreType.DMA((len(pieces),)),
             ],
         ),
         out_shape=[jax.ShapeDtypeStruct((tokens, 2 * DV), F32)] * 3
@@ -205,7 +212,7 @@
             flops=3 * 10**10, bytes_accessed=2 * 10**7, transcendentals=0
         ),
         name="delta_local",
-    )(place, *firsts, *seconds, *weights, cumulative, rates)
+    )(place, *pieces, *weights, cumulative, rates)
 
 
 def gate_kernel(
@@ -363,16 +370,20 @@
     return plus(groups(0), from_behind, from_ahead).astype(final)
 
 
+def direct_sums(terms, axis):
+    far = neighbour(terms[2], axis, 2)
+    behind = neighbour(terms[1], axis, 1)
+    ahead = neighbour(terms[3], axis, -1)
+    return plus(terms[0], behind, ahead, far)
+
+
 def scatter_sums(first, second):
     up_a, down_a = far_sums(first, 0)
     up_b, down_b = far_sums(second, 1)
     up_a, down_a, up_b, down_b = lax.optimization_barrier((up_a, down_a, up_b, down_b))
     a = near_sums(first, 0, up_a, down_a, BF16)
     b = near_sums(second, 1, up_b, down_b, BF16)
-    first, second = (lambda k: a[k % SIDE]), (lambda k: b[k % SIDE])
-    a_last = near_sums(first, 1, *far_sums(first, 1), F32)
-    b_last = near_sums(second, 0, *far_sums(second, 0), F32)
-    return jnp.concatenate([a_last, b_last], axis=0)
+    return jnp.concatenate([direct_sums(a, 1), direct_sums(b, 0)], axis=0)
 
 
 def gather_direct(block, axis):
@@ -393,13 +404,12 @@
     half = a.shape[0] // 2
     a_behind, a_ahead = neighbour(a, 0, 1), neighbour(a, 0, -1)
     b_behind, b_ahead = neighbour(b, 1, 1), neighbour(b, 1, -1)
-    a_behind, a_ahead, b_behind, b_ahead, beside = tie(
-        (a_behind, a_ahead, b_behind, b_ahead, beside)
-    )
+    a_behind, a_ahead, b_behind, b_ahead = tie((a_behind, a_ahead, b_behind, b_ahead))
     a_far = (neighbour(a_behind[:half], 0, 1), neighbour(a_ahead[half:], 0, -1))
     b_far = (neighbour(b_behind[:half], 1, 1), neighbour(b_ahead[half:], 1, -1))
-    first = [a, a_ahead, jnp.concatenate(a_far, axis=0), a_behind]
-    second = [b, b_ahead, jnp.concatenate(b_far, axis=0), b_behind]
+    a_far, b_far, beside = tie((a_far, b_far, beside))
+    first = [(a,), (a_ahead,), a_far, (a_behind,)]
+    second = [(b,), (b_ahead,), b_far, (b_behind,)]
     return first, second, beside
 
 
@@ -497,7 +507,7 @@
     made = {}
     previous = None
     for k in (0, 1, 2, 3):
-        xa, xb = rows_first[k], rows_second[k]
+        xa, xb = jnp.concatenate(rows_first[k]), jnp.concatenate(rows_second[k])
         if previous is None:
             xa, xb, shared = lax.optimization_barrier((xa, xb, shared))
         else:

time: 350 us -> 337 us (0.963)
  starting transfers between devices: 78.7 us -> 71.7 us
  waiting for transfers between devices: 85.6 us -> 92.4 us
  other arithmetic: 20.3 us -> 14.6 us
  local copies, waits for them, and re-layouts: 21.9 us -> 17.8 us
    ppermute x44 -> x42, waiting for transfers between devices: 78.7 us -> 85.5 us  [neighbour(): return lax.ppermute(value, 'exp', pairs)]
    ppermute x44 -> x42, starting transfers between devices: 69.4 us -> 62.7 us  [neighbour(): return lax.ppermute(value, 'exp', pairs)]
    concatenate x4 -> x2, other arithmetic: 4.77 us -> 0.19 us  [local(): xa, xb = (jnp.concatenate(rows_first[k]), jnp.concatenate(rows_second[k]))]
    slice x4, local copies, waits for them, and re-layouts: 6 us -> 2.29 us  [gather_rows(): b_far = (neighbour(b_behind[:half], 1, 1), neighbour(b_ahead[half:], 1, -1))]
  transfers between devices with their start and end apart: 51 -> 49, of which waited for: 25 -> 25; matrix products, arithmetic and copies ran while one was open for 11% -> 9% of each run, Pallas kernels for 22% -> 22%
where the time goes in v2:
time: 337 us; the launch traced here: 332 us
  waiting for transfers between devices  92.4 us (27%)
  Pallas kernels  84.7 us (25%)
  starting transfers between devices  71.7 us (21%)
  blocking collectives  23.9 us (7%)
  local copies, waits for them, and re-layouts  17.8 us (5%)
  between operations  14.8 us (4%)
  other arithmetic  14.6 us (4%)
  matrix products  11.6 us (3%)
    ppermute x42, waiting for transfers between devices, neighbour(): return lax.ppermute(value, 'exp', pairs)  85.5 us
    ppermute x42, starting transfers between devices, neighbour(): return lax.ppermute(value, 'exp', pairs)  62.7 us
    pallas_call x4, Pallas kernels, expert_mix(): pl.pallas_call(expert_kernel, grid=(count * EXPERT_CUTS,), in_specs=[rows...  46.1 us
    pallas_call x1, Pallas kernels, delta_local(): pl.pallas_call(lambda *refs: delta_kernel(blocks, spots, *refs), grid_spe...  31.6 us
    all_to_all x1, blocking collectives, local(): lax.all_to_all(gated.reshape(owners, tok_dev, -1), 'exp', split_axis=0, c...  23.9 us
    ppermute x6, starting transfers between devices, along_seq(): return lax.ppermute(value, 'seq', pairs)  8.93 us
    pallas_call x1, Pallas kernels, delta_gate(): pl.pallas_call(gate_kernel, grid_spec=pltpu.PrefetchScalarGridSpec(num_sc...  6.96 us
    ppermute x6, waiting for transfers between devices, along_seq(): return lax.ppermute(value, 'seq', pairs)  6.88 us
  transfers between devices with their start and end apart: 49, of which 25 were waited for; matrix products, arithmetic and copies ran while one was open for 9% of the time, Pallas kernels for 22%

profile of v2, /device:TPU:32, one launch (start us, length us, event | category | flops | bytes accessed | tf_op | source)
XLA Modules:
  0.0 331.5 jit_solution(9055252818777293636)
XLA Ops:
  9.2 2.8 collective-permute-start
  13.7 3.0 collective-permute-start.3
  17.4 5.9 %collective-permute-done = bf16[64,2048]{1,0:T(8,128)(2,1)S(1)} collective-permute-done((bf16[64,2048]{1,0:T(8,128)(2,1)S(1)}, bf16[64,2048]{1,0:T(8,128)(2,1)S(1)}, u32[]{:S(2)}, u32[]{:S(2)}) %collective-permute-start) | collective-permute-done | bytes 262176 | tf_op jit(solution)/shard_map/ppermute | solution.py:347
  23.3 1.6 collective-permute-start.5
  24.8 2.1 collective-permute-done.2
  27.5 3.3 %collective-permute-done.5 = bf16[64,2048]{1,0:T(8,128)(2,1)S(1)} collective-permute-done((bf16[64,2048]{1,0:T(8,128)(2,1)S(1)}, bf16[64,2048]{1,0:T(8,128)(2,1)S(1)}, u32[]{:S(2)}, u32[]{:S(2)}) %collective-permute-start.5) | collective-permute-done | bytes 262176 | tf_op jit(solution)/shard_map/ppermute | solution.py:347
  31.0 1.8 collective-permute-start.8
  32.8 2.9 collective-permute-start.9
  36.2 2.9 collective-permute-start.7
  39.1 17.9 %collective-permute-done.8.refs_10_ = bf16[4,64,2048]{2,1,0:T(8,128)(2,1)S(1)} collective-permute-done((bf16[4,64,2048]{2,1,0:T(8,128)(2,1)S(1)}, bf16[4,64,2048]{2,1,0:T(8,128)(2,1)S(1)}, u32[]{:S(2)}, u32[]{:S(2)}) %collective-permute-start.8) | collective-permute-done | bytes 1048608 | tf_op jit(solution)/shard_map/ppermute | solution.py:347
  57.6 2.4 collective-permute-done.6.refs_5_
  62.0 2.9 collective-permute-start.11
  66.0 3.0 collective-permute-start.13
  68.9 1.9 constant_dynamic-slice_fusion
  70.8 2.3 collective-permute-done.10.refs_3_
  73.3 3.3 %collective-permute-done.12.refs_8_ = bf16[2,64,2048]{2,1,0:T(8,128)(2,1)} collective-permute-done((bf16[2,64,2048]{2,1,0:T(8,128)(2,1)S(1)}, bf16[2,64,2048]{2,1,0:T(8,128)(2,1)}, u32[]{:S(2)}, u32[]{:S(2)}) %collective-permute-start.12) | collective-permute-done | bytes 524320 | tf_op jit(solution)/shard_map/ppermute | solution.py:347
  76.6 1.6 collective-permute-done.13.refs_9_
  80.6 31.6 %delta_local.1 = (f32[2048,256]{1,0:T(8,128)}, f32[2048,256]{1,0:T(8,128)}, f32[2048,256]{1,0:T(8,128)}, f32[2,128,256]{2,1,0:T(8,128)}) custom-call(s32[3]{0:T(128)} %pad_add_fusion.refs_0_.place_ref, bf16[4,64,2048]{2,1,0:T(8,128)(2,1)} %copy-done.20, bf16[4,64,2048]{2,1,0:T(8,128)(2,1)} %copy-done.24, ...), custom_call_target="tpu_custom_call" | custom-call | flops 30000001024 | bytes 20000000 | tf_op jit(solution)/shard_map/delta_local/pallas_call | solution.py:185
  116.6 5.6 %collective-permute-start.16 = (bf16[2,128,256]{2,1,0:T(8,128)(2,1)S(1)}, bf16[2,128,256]{2,1,0:T(8,128)(2,1)S(1)}, u32[]{:S(2)}, u32[]{:S(2)}) collective-permute-start(bf16[2,128,256]{2,1,0:T(8,128)(2,1)S(1)} %pad_maximum_fusion.11), channel_id=1, source_target_pairs={{0,64},{16,80},{32,96},{48,112},{1,65},{17,81},{33,97},{49,113},{2... | collective-permute-start | bytes 393224 | tf_op jit(solution)/shard_map/ppermute | solution.py:417
  122.2 1.9 collective-permute-start.17
  125.2 4.4 %collective-permute-done.17 = bf16[2,128,256]{2,1,0:T(8,128)(2,1)S(1)} collective-permute-done((bf16[2,128,256]{2,1,0:T(8,128)(2,1)S(1)}, bf16[2,128,256]{2,1,0:T(8,128)(2,1)S(1)}, u32[]{:S(2)}, u32[]{:S(2)}) %collective-permute-start.17) | collective-permute-done | bytes 131104 | tf_op jit(solution)/shard_map/ppermute | solution.py:417
  130.5 7.0 %delta_gate.1 = bf16[2048,256]{1,0:T(8,128)(2,1)} custom-call(s32[3]{0:T(128)} %pad_add_fusion.refs_0_.place_ref, bf16[4,2,128,256]{3,2,1,0:T(8,128)(2,1)} %pad_maximum_fusion.10.maps_ref, f32[2048,256]{1,0:T(8,128)} %get-tuple-element.70.base_ref, f32[2048,256]{1,0:T(8,128)} %get-tuple-element.71.reach_ref, f32[2048,256]{1,0:T(8,128)} %get-tuple-element.72.gate_ref, ...), custom_call_target="tpu_custom_call" | custom-call | flops 1000000000 | bytes 10000000 | tf_op jit(solution)/shard_map/delta_gate/pallas_call | solution.py:247
  137.5 23.9 %all_to_all.5 = bf16[16,128,256]{2,1,0:T(8,128)(2,1)S(1)} all-to-all(bf16[16,128,256]{2,1,0:T(8,128)(2,1)} %bitcast.112), channel_id=1, replica_groups=mesh['seq'=8,'exp'=16] {'exp'}, dimensions={0} | all-to-all | bytes 2097152 | tf_op jit(solution)/shard_map/all_to_all | solution.py:480
  166.0 5.1 %fusion = bf16[128,1024]{1,0:T(8,128)(2,1)S(1)} fusion(bf16[16,128,256]{2,1,0:T(8,128)(2,1)} %collective-permute-done.18, bf16[16,256,1024]{2,1,0:T(8,128)(2,1)} %bitcast.110), kind=kOutput, calls=%fused_computation.12 | convolution fusion | flops 1073872896 | bytes 9699328 | tf_op jit(solution)/shard_map/stc,scd->td/dot_general | solution.py:484
  181.6 2.6 collective-permute-done.23
  186.0 2.2 collective-permute-done.24
  188.2 4.9 %collective-permute-done.25 = bf16[64,2048]{1,0:T(8,128)(2,1)S(1)} collective-permute-done((bf16[64,2048]{1,0:T(8,128)(2,1)S(1)}, bf16[64,2048]{1,0:T(8,128)(2,1)S(1)}, u32[]{:S(2)}, u32[]{:S(2)}) %collective-permute-start.25) | collective-permute-done | bytes 262176 | tf_op jit(solution)/shard_map/ppermute | solution.py:347
  196.4 2.7 collective-permute-start.26
  199.5 3.6 %convolution_multiply_fusion = f32[128,2048]{1,0:T(8,128)} fusion(bf16[512,2048]{1,0:T(8,128)(2,1)S(1)} %copy-done, bf16[128,2048]{1,0:T(8,128)(2,1)} %copy-done.8, bf16[2048,512]{1,0:T(8,128)(2,1)} %param.37, f32[128]{0:T(128)S(1)} %fusion.5, f32[128,512]{1,0:T(8,128)} %fusion.32), kind=kOutput, calls=%fused_computation | convolution fusion | flops 537526272 | bytes 6029824 | tf_op jit(solution)/shard_map/dot_general | solution.py:498
  204.9 11.5 %expert_mix.4 = (bf16[4,64,2048]{2,1,0:T(8,128)(2,1)S(1)}, bf16[4,64,2048]{2,1,0:T(8,128)(2,1)S(1)}) custom-call(bf16[4,64,2048]{2,1,0:T(8,128)(2,1)} %pad_maximum_fusion.2.xa_ref, bf16[4,64,2048]{2,1,0:T(8,128)(2,1)S(1)} %pad_maximum_fusion.3.xb_ref, f32[4,64,2]{2,1,0:T(8,128)S(1)} %copy-done.6, f32[4,64,2]{2,1,0:T(8,128)S(1)} %copy-done.5, ...), custom_call_target="tpu_custom_call" | custom-call | flops 6442450944 | bytes 16777216 | tf_op jit(solution)/shard_map/expert_mix/pallas_call | solution.py:318
  216.5 2.0 collective-permute-done.27.xb_ref
  218.5 3.4 %collective-permute-done.26.xa_ref = bf16[4,64,2048]{2,1,0:T(8,128)(2,1)} collective-permute-done((bf16[4,64,2048]{2,1,0:T(8,128)(2,1)}, bf16[4,64,2048]{2,1,0:T(8,128)(2,1)}, u32[]{:S(2)}, u32[]{:S(2)}) %collective-permute-start.26) | collective-permute-done | bytes 1048608 | tf_op jit(solution)/shard_map/ppermute | solution.py:347
  224.2 3.3 collective-permute-start.33
  230.9 2.6 collective-permute-start.30
  233.5 11.9 %expert_mix.5 = (bf16[4,64,2048]{2,1,0:T(8,128)(2,1)S(1)}, bf16[4,64,2048]{2,1,0:T(8,128)(2,1)S(1)}) custom-call(bf16[4,64,2048]{2,1,0:T(8,128)(2,1)} %collective-permute-done.26.xa_ref, bf16[4,64,2048]{2,1,0:T(8,128)(2,1)} %collective-permute-done.27.xb_ref, f32[4,64,2]{2,1,0:T(8,128)S(1)} %copy-done.4, f32[4,64,2]{2,1,0:T(8,128)S(1)} %copy-done.3, ...), custom_call_target="tpu_custom_call" | custom-call | flops 6442450944 | bytes 16777216 | tf_op jit(solution)/shard_map/expert_mix/pallas_call | solution.py:318
  246.3 10.9 %expert_mix.6 = (bf16[4,64,2048]{2,1,0:T(8,128)(2,1)S(1)}, bf16[4,64,2048]{2,1,0:T(8,128)(2,1)S(1)}) custom-call(bf16[4,64,2048]{2,1,0:T(8,128)(2,1)S(1)} %pad_maximum_fusion.4.xa_ref, bf16[4,64,2048]{2,1,0:T(8,128)(2,1)S(1)} %pad_maximum_fusion.5.xb_ref, f32[4,64,2]{2,1,0:T(8,128)S(1)} %copy-done.2, f32[4,64,2]{2,1,0:T(8,128)S(1)} %get-tuple-element.116.sb_ref, ...), custom_call_target="tpu_custom_call" | custom-call | flops 6442450944 | bytes 16777216 | tf_op jit(solution)/shard_map/expert_mix/pallas_call | solution.py:318
  257.4 3.2 collective-permute-start.35
  261.0 3.2 collective-permute-start.37
  264.3 11.9 %expert_mix.7 = (bf16[4,64,2048]{2,1,0:T(8,128)(2,1)S(1)}, bf16[4,64,2048]{2,1,0:T(8,128)(2,1)S(1)}) custom-call(bf16[4,64,2048]{2,1,0:T(8,128)(2,1)} %collective-permute-done.28.xa_ref, bf16[4,64,2048]{2,1,0:T(8,128)(2,1)} %collective-permute-done.31.xb_ref, f32[4,64,2]{2,1,0:T(8,128)S(1)} %get-tuple-element.119.sa_ref, ...), custom_call_target="tpu_custom_call" | custom-call | flops 6442450944 | bytes 16777216 | tf_op jit(solution)/shard_map/expert_mix/pallas_call | solution.py:318
  276.9 3.3 collective-permute-start.39
  280.8 3.3 collective-permute-start.44
  284.1 16.0 %collective-permute-done.38 = bf16[4,64,2048]{2,1,0:T(8,128)(2,1)S(1)} collective-permute-done((bf16[4,64,2048]{2,1,0:T(8,128)(2,1)S(1)}, bf16[4,64,2048]{2,1,0:T(8,128)(2,1)S(1)}, u32[]{:S(2)}, u32[]{:S(2)}) %collective-permute-start.38) | collective-permute-done | bytes 1048608 | tf_op jit(solution)/shard_map/ppermute | solution.py:347
  300.7 3.2 collective-permute-start.41
  304.0 3.0 collective-permute-done.43
  307.7 3.2 collective-permute-start.46
  310.9 3.7 %collective-permute-done.40 = bf16[64,2048]{1,0:T(8,128)(2,1)S(1)} collective-permute-done((bf16[64,2048]{1,0:T(8,128)(2,1)S(1)}, bf16[64,2048]{1,0:T(8,128)(2,1)S(1)}, u32[]{:S(2)}, u32[]{:S(2)}) %collective-permute-start.40) | collective-permute-done | bytes 262176 | tf_op jit(solution)/shard_map/ppermute | solution.py:347
  314.7 3.1 collective-permute-done.45
  317.9 4.6 %collective-permute-done.47 = bf16[64,2048]{1,0:T(8,128)(2,1)S(1)} collective-permute-done((bf16[64,2048]{1,0:T(8,128)(2,1)S(1)}, bf16[64,2048]{1,0:T(8,128)(2,1)S(1)}, u32[]{:S(2)}, u32[]{:S(2)}) %collective-permute-start.47) | collective-permute-done | bytes 262176 | tf_op jit(solution)/shard_map/ppermute | solution.py:347
  (191 shorter events, 52.5 us)
Async XLA Ops:
  6.5 159.5 %all-gather.3.cloned.1.call-start = ((), (), s32[]{:S(2)}) async-start(), calls=%async_computation.1 | async-start | bytes 8912896 | tf_op jit(solution)/shard_map/all_gather | solution.py:471
  9.2 14.0 %collective-permute-start = (bf16[64,2048]{1,0:T(8,128)(2,1)S(1)}, bf16[64,2048]{1,0:T(8,128)(2,1)S(1)}, u32[]{:S(2)}, u32[]{:S(2)}) collective-permute-start(bf16[64,2048]{1,0:T(8,128)(2,1)S(1)} %get-tuple-element.53), channel_id=1, source_target_pairs={{0,3},{1,0},{2,1},{3,2},{4,7},{5,4},{6,5},{7,6},{8,11},{9,8},{10,9... | collective-permute-start | bytes 786440 | tf_op jit(solution)/shard_map/ppermute | solution.py:347
  12.0 12.8 %collective-permute-start.1 = (bf16[64,2048]{1,0:T(8,128)(2,1)S(1)}, bf16[64,2048]{1,0:T(8,128)(2,1)S(1)}, u32[]{:S(2)}, u32[]{:S(2)}) collective-permute-start(bf16[64,2048]{1,0:T(8,128)(2,1)S(1)} %get-tuple-element.53), channel_id=1, source_target_pairs={{0,2},{1,3},{2,0},{3,1},{4,6},{5,7},{6,4},{7,5},{8,10},{9,11},{10,... | collective-permute-start | bytes 786440 | tf_op jit(solution)/shard_map/ppermute | solution.py:347
  12.8 14.1 %collective-permute-start.2 = (bf16[64,2048]{1,0:T(8,128)(2,1)S(1)}, bf16[64,2048]{1,0:T(8,128)(2,1)S(1)}, u32[]{:S(2)}, u32[]{:S(2)}) collective-permute-start(bf16[64,2048]{1,0:T(8,128)(2,1)S(1)} %get-tuple-element.53), channel_id=1, source_target_pairs={{0,1},{1,2},{2,3},{3,0},{4,5},{5,6},{6,7},{7,4},{8,9},{9,10},{10,1... | collective-permute-start | bytes 786440 | tf_op jit(solution)/shard_map/ppermute | solution.py:347
  13.7 13.4 %collective-permute-start.3 = (bf16[64,2048]{1,0:T(8,128)(2,1)S(1)}, bf16[64,2048]{1,0:T(8,128)(2,1)S(1)}, u32[]{:S(2)}, u32[]{:S(2)}) collective-permute-start(bf16[64,2048]{1,0:T(8,128)(2,1)S(1)} %get-tuple-element.57), channel_id=1, source_target_pairs={{0,12},{1,13},{2,14},{3,15},{4,0},{5,1},{6,2},{7,3},{8,4},{9,5},{1... | collective-permute-start | bytes 786440 | tf_op jit(solution)/shard_map/ppermute | solution.py:347
  16.7 10.8 %collective-permute-start.4 = (bf16[64,2048]{1,0:T(8,128)(2,1)S(1)}, bf16[64,2048]{1,0:T(8,128)(2,1)S(1)}, u32[]{:S(2)}, u32[]{:S(2)}) collective-permute-start(bf16[64,2048]{1,0:T(8,128)(2,1)S(1)} %get-tuple-element.57), channel_id=1, source_target_pairs={{0,8},{1,9},{2,10},{3,11},{4,12},{5,13},{6,14},{7,15},{8,0},{9,1},... | collective-permute-start | bytes 786440 | tf_op jit(solution)/shard_map/ppermute | solution.py:347
  23.3 7.6 %collective-permute-start.5 = (bf16[64,2048]{1,0:T(8,128)(2,1)S(1)}, bf16[64,2048]{1,0:T(8,128)(2,1)S(1)}, u32[]{:S(2)}, u32[]{:S(2)}) collective-permute-start(bf16[64,2048]{1,0:T(8,128)(2,1)S(1)} %get-tuple-element.57), channel_id=1, source_target_pairs={{0,4},{1,5},{2,6},{3,7},{4,8},{5,9},{6,10},{7,11},{8,12},{9,13},{1... | collective-permute-start | bytes 786440 | tf_op jit(solution)/shard_map/ppermute | solution.py:347
  31.0 26.0 %collective-permute-start.8 = (bf16[4,64,2048]{2,1,0:T(8,128)(2,1)S(1)}, bf16[4,64,2048]{2,1,0:T(8,128)(2,1)S(1)}, u32[]{:S(2)}, u32[]{:S(2)}) collective-permute-start(bf16[4,64,2048]{2,1,0:T(8,128)(2,1)S(1)} %pad_maximum_fusion.1.refs_6_), channel_id=1, source_target_pairs={{0,1},{1,2},{2,3},{3,0},{4,5},{5,6},{6,7},{7,4},{8,9},{9,10},{10,1... | collective-permute-start | bytes 3145736 | tf_op jit(solution)/shard_map/ppermute | solution.py:347
  32.8 24.8 %collective-permute-start.9 = (bf16[4,64,2048]{2,1,0:T(8,128)(2,1)S(1)}, bf16[4,64,2048]{2,1,0:T(8,128)(2,1)S(1)}, u32[]{:S(2)}, u32[]{:S(2)}) collective-permute-start(bf16[4,64,2048]{2,1,0:T(8,128)(2,1)S(1)} %pad_maximum_fusion.1.refs_6_), channel_id=1, source_target_pairs={{0,3},{1,0},{2,1},{3,2},{4,7},{5,4},{6,5},{7,6},{8,11},{9,8},{10,9... | collective-permute-start | bytes 3145736 | tf_op jit(solution)/shard_map/ppermute | solution.py:347
  35.8 24.2 %collective-permute-start.6 = (bf16[4,64,2048]{2,1,0:T(8,128)(2,1)S(1)}, bf16[4,64,2048]{2,1,0:T(8,128)(2,1)S(1)}, u32[]{:S(2)}, u32[]{:S(2)}) collective-permute-start(bf16[4,64,2048]{2,1,0:T(8,128)(2,1)S(1)} %pad_maximum_fusion.refs_1_), channel_id=1, source_target_pairs={{0,4},{1,5},{2,6},{3,7},{4,8},{5,9},{6,10},{7,11},{8,12},{9,13},{1... | collective-permute-start | bytes 3145736 | tf_op jit(solution)/shard_map/ppermute | solution.py:347
  36.2 23.8 %collective-permute-start.7 = (bf16[4,64,2048]{2,1,0:T(8,128)(2,1)S(1)}, bf16[4,64,2048]{2,1,0:T(8,128)(2,1)S(1)}, u32[]{:S(2)}, u32[]{:S(2)}) collective-permute-start(bf16[4,64,2048]{2,1,0:T(8,128)(2,1)S(1)} %pad_maximum_fusion.refs_1_), channel_id=1, source_target_pairs={{0,12},{1,13},{2,14},{3,15},{4,0},{5,1},{6,2},{7,3},{8,4},{9,5},{1... | collective-permute-start | bytes 3145736 | tf_op jit(solution)/shard_map/ppermute | solution.py:347
  60.9 12.3 %collective-permute-start.10 = (bf16[2,64,2048]{2,1,0:T(8,128)(2,1)}, bf16[2,64,2048]{2,1,0:T(8,128)(2,1)}, u32[]{:S(2)}, u32[]{:S(2)}) collective-permute-start(bf16[2,64,2048]{2,1,0:T(8,128)(2,1)} %slice.141), channel_id=1, source_target_pairs={{0,4},{1,5},{2,6},{3,7},{4,8},{5,9},{6,10},{7,11},{8,12},{9,13},{1... | collective-permute-start | bytes 1572872 | tf_op jit(solution)/shard_map/ppermute | solution.py:347
  62.0 11.2 %collective-permute-start.11 = (bf16[2,64,2048]{2,1,0:T(8,128)(2,1)}, bf16[2,64,2048]{2,1,0:T(8,128)(2,1)}, u32[]{:S(2)}, u32[]{:S(2)}) collective-permute-start(bf16[2,64,2048]{2,1,0:T(8,128)(2,1)} %slice.142), channel_id=1, source_target_pairs={{0,12},{1,13},{2,14},{3,15},{4,0},{5,1},{6,2},{7,3},{8,4},{9,5},{1... | collective-permute-start | bytes 1572872 | tf_op jit(solution)/shard_map/ppermute | solution.py:347
  65.0 11.6 %collective-permute-start.12 = (bf16[2,64,2048]{2,1,0:T(8,128)(2,1)S(1)}, bf16[2,64,2048]{2,1,0:T(8,128)(2,1)}, u32[]{:S(2)}, u32[]{:S(2)}) collective-permute-start(bf16[2,64,2048]{2,1,0:T(8,128)(2,1)S(1)} %slice.143), channel_id=1, source_target_pairs={{0,1},{1,2},{2,3},{3,0},{4,5},{5,6},{6,7},{7,4},{8,9},{9,10},{10,1... | collective-permute-start | bytes 1572872 | tf_op jit(solution)/shard_map/ppermute | solution.py:347
  66.0 12.2 %collective-permute-start.13 = (bf16[2,64,2048]{2,1,0:T(8,128)(2,1)S(1)}, bf16[2,64,2048]{2,1,0:T(8,128)(2,1)}, u32[]{:S(2)}, u32[]{:S(2)}) collective-permute-start(bf16[2,64,2048]{2,1,0:T(8,128)(2,1)S(1)} %slice.144), channel_id=1, source_target_pairs={{0,3},{1,0},{2,1},{3,2},{4,7},{5,4},{6,5},{7,6},{8,11},{9,8},{10,9... | collective-permute-start | bytes 1572872 | tf_op jit(solution)/shard_map/ppermute | solution.py:347
  115.9 8.2 %collective-permute-start.15 = (bf16[2,128,256]{2,1,0:T(8,128)(2,1)S(1)}, bf16[2,128,256]{2,1,0:T(8,128)(2,1)S(1)}, u32[]{:S(2)}, u32[]{:S(2)}) collective-permute-start(bf16[2,128,256]{2,1,0:T(8,128)(2,1)S(1)} %pad_maximum_fusion.11), channel_id=1, source_target_pairs={{0,96},{16,112},{1,97},{17,113},{2,98},{18,114},{3,99},{19,115},{4... | collective-permute-start | bytes 393224 | tf_op jit(solution)/shard_map/ppermute | solution.py:417
  116.6 8.7 %collective-permute-start.16 = (bf16[2,128,256]{2,1,0:T(8,128)(2,1)S(1)}, bf16[2,128,256]{2,1,0:T(8,128)(2,1)S(1)}, u32[]{:S(2)}, u32[]{:S(2)}) collective-permute-start(bf16[2,128,256]{2,1,0:T(8,128)(2,1)S(1)} %pad_maximum_fusion.11), channel_id=1, source_target_pairs={{0,64},{16,80},{32,96},{48,112},{1,65},{17,81},{33,97},{49,113},{2... | collective-permute-start | bytes 393224 | tf_op jit(solution)/shard_map/ppermute | solution.py:417
  122.2 7.5 %collective-permute-start.17 = (bf16[2,128,256]{2,1,0:T(8,128)(2,1)S(1)}, bf16[2,128,256]{2,1,0:T(8,128)(2,1)S(1)}, u32[]{:S(2)}, u32[]{:S(2)}) collective-permute-start(bf16[2,128,256]{2,1,0:T(8,128)(2,1)S(1)} %pad_maximum_fusion.11), channel_id=1, source_target_pairs={{0,32},{16,48},{32,64},{48,80},{64,96},{80,112},{1,33},{17,49},{33... | collective-permute-start | bytes 393224 | tf_op jit(solution)/shard_map/ppermute | solution.py:417
  161.4 4.6 %collective-permute-start.18 = (bf16[16,128,256]{2,1,0:T(8,128)(2,1)S(1)}, bf16[16,128,256]{2,1,0:T(8,128)(2,1)}, u32[]{:S(2)}, u32[]{:S(2)}) collective-permute-start(bf16[16,128,256]{2,1,0:T(8,128)(2,1)S(1)} %all_to_all.5), channel_id=1, source_target_pairs={{0,16},{16,0},{32,48},{48,32},{64,80},{80,64},{96,112},{112,96},{1... | collective-permute-start | bytes 3145736 | tf_op jit(solution)/shard_map/ppermute | solution.py:417
  171.1 2.4 collective-permute-start.19
  175.1 9.2 %collective-permute-start.23 = (bf16[64,2048]{1,0:T(8,128)(2,1)S(1)}, bf16[64,2048]{1,0:T(8,128)(2,1)S(1)}, u32[]{:S(2)}, u32[]{:S(2)}) collective-permute-start(bf16[64,2048]{1,0:T(8,128)(2,1)S(1)} %get-tuple-element.125), channel_id=1, source_target_pairs={{0,12},{1,13},{2,14},{3,15},{4,0},{5,1},{6,2},{7,3},{8,4},{9,5},{1... | collective-permute-start | bytes 786440 | tf_op jit(solution)/shard_map/ppermute | solution.py:347
  177.5 10.7 %collective-permute-start.24 = (bf16[64,2048]{1,0:T(8,128)(2,1)S(1)}, bf16[64,2048]{1,0:T(8,128)(2,1)S(1)}, u32[]{:S(2)}, u32[]{:S(2)}) collective-permute-start(bf16[64,2048]{1,0:T(8,128)(2,1)S(1)} %get-tuple-element.125), channel_id=1, source_target_pairs={{0,8},{1,9},{2,10},{3,11},{4,12},{5,13},{6,14},{7,15},{8,0},{9,1},... | collective-permute-start | bytes 786440 | tf_op jit(solution)/shard_map/ppermute | solution.py:347
  178.2 14.9 %collective-permute-start.25 = (bf16[64,2048]{1,0:T(8,128)(2,1)S(1)}, bf16[64,2048]{1,0:T(8,128)(2,1)S(1)}, u32[]{:S(2)}, u32[]{:S(2)}) collective-permute-start(bf16[64,2048]{1,0:T(8,128)(2,1)S(1)} %get-tuple-element.125), channel_id=1, source_target_pairs={{0,4},{1,5},{2,6},{3,7},{4,8},{5,9},{6,10},{7,11},{8,12},{9,13},{1... | collective-permute-start | bytes 786440 | tf_op jit(solution)/shard_map/ppermute | solution.py:347
  179.0 16.3 %collective-permute-start.20 = (bf16[64,2048]{1,0:T(8,128)(2,1)S(1)}, bf16[64,2048]{1,0:T(8,128)(2,1)S(1)}, u32[]{:S(2)}, u32[]{:S(2)}) collective-permute-start(bf16[64,2048]{1,0:T(8,128)(2,1)S(1)} %get-tuple-element.126), channel_id=1, source_target_pairs={{0,3},{1,0},{2,1},{3,2},{4,7},{5,4},{6,5},{7,6},{8,11},{9,8},{10,9... | collective-permute-start | bytes 786440 | tf_op jit(solution)/shard_map/ppermute | solution.py:347
  180.2 15.1 %collective-permute-start.21 = (bf16[64,2048]{1,0:T(8,128)(2,1)S(1)}, bf16[64,2048]{1,0:T(8,128)(2,1)S(1)}, u32[]{:S(2)}, u32[]{:S(2)}) collective-permute-start(bf16[64,2048]{1,0:T(8,128)(2,1)S(1)} %get-tuple-element.126), channel_id=1, source_target_pairs={{0,2},{1,3},{2,0},{3,1},{4,6},{5,7},{6,4},{7,5},{8,10},{9,11},{10,... | collective-permute-start | bytes 786440 | tf_op jit(solution)/shard_map/ppermute | solution.py:347
  184.3 11.0 %collective-permute-start.22 = (bf16[64,2048]{1,0:T(8,128)(2,1)S(1)}, bf16[64,2048]{1,0:T(8,128)(2,1)S(1)}, u32[]{:S(2)}, u32[]{:S(2)}) collective-permute-start(bf16[64,2048]{1,0:T(8,128)(2,1)S(1)} %get-tuple-element.126), channel_id=1, source_target_pairs={{0,1},{1,2},{2,3},{3,0},{4,5},{5,6},{6,7},{7,4},{8,9},{9,10},{10,1... | collective-permute-start | bytes 786440 | tf_op jit(solution)/shard_map/ppermute | solution.py:347
  193.2 25.3 %collective-permute-start.27 = (bf16[4,64,2048]{2,1,0:T(8,128)(2,1)S(1)}, bf16[4,64,2048]{2,1,0:T(8,128)(2,1)}, u32[]{:S(2)}, u32[]{:S(2)}) collective-permute-start(bf16[4,64,2048]{2,1,0:T(8,128)(2,1)S(1)} %pad_maximum_fusion.3.xb_ref), channel_id=1, source_target_pairs={{0,3},{1,0},{2,1},{3,2},{4,7},{5,4},{6,5},{7,6},{8,11},{9,8},{10,9... | collective-permute-start | bytes 3145736 | tf_op jit(solution)/shard_map/ppermute | solution.py:347
  194.1 27.8 %collective-permute-start.31 = (bf16[4,64,2048]{2,1,0:T(8,128)(2,1)S(1)}, bf16[4,64,2048]{2,1,0:T(8,128)(2,1)}, u32[]{:S(2)}, u32[]{:S(2)}) collective-permute-start(bf16[4,64,2048]{2,1,0:T(8,128)(2,1)S(1)} %pad_maximum_fusion.3.xb_ref), channel_id=1, source_target_pairs={{0,1},{1,2},{2,3},{3,0},{4,5},{5,6},{6,7},{7,4},{8,9},{9,10},{10,1... | collective-permute-start | bytes 3145736 | tf_op jit(solution)/shard_map/ppermute | solution.py:347
  196.4 25.5 %collective-permute-start.26 = (bf16[4,64,2048]{2,1,0:T(8,128)(2,1)}, bf16[4,64,2048]{2,1,0:T(8,128)(2,1)}, u32[]{:S(2)}, u32[]{:S(2)}) collective-permute-start(bf16[4,64,2048]{2,1,0:T(8,128)(2,1)} %pad_maximum_fusion.2.xa_ref), channel_id=1, source_target_pairs={{0,12},{1,13},{2,14},{3,15},{4,0},{5,1},{6,2},{7,3},{8,4},{9,5},{1... | collective-permute-start | bytes 3145736 | tf_op jit(solution)/shard_map/ppermute | solution.py:347
  199.1 28.4 %collective-permute-start.28 = (bf16[4,64,2048]{2,1,0:T(8,128)(2,1)}, bf16[4,64,2048]{2,1,0:T(8,128)(2,1)}, u32[]{:S(2)}, u32[]{:S(2)}) collective-permute-start(bf16[4,64,2048]{2,1,0:T(8,128)(2,1)} %pad_maximum_fusion.2.xa_ref), channel_id=1, source_target_pairs={{0,4},{1,5},{2,6},{3,7},{4,8},{5,9},{6,10},{7,11},{8,12},{9,13},{1... | collective-permute-start | bytes 3145736 | tf_op jit(solution)/shard_map/ppermute | solution.py:347
  223.0 22.4 %collective-permute-start.32 = (bf16[2,64,2048]{2,1,0:T(8,128)(2,1)S(1)}, bf16[2,64,2048]{2,1,0:T(8,128)(2,1)S(1)}, u32[]{:S(2)}, u32[]{:S(2)}) collective-permute-start(bf16[2,64,2048]{2,1,0:T(8,128)(2,1)S(1)} %slice.199), channel_id=1, source_target_pairs={{0,1},{1,2},{2,3},{3,0},{4,5},{5,6},{6,7},{7,4},{8,9},{9,10},{10,1... | collective-permute-start | bytes 1572872 | tf_op jit(solution)/shard_map/ppermute | solution.py:347
  224.2 21.2 %collective-permute-start.33 = (bf16[2,64,2048]{2,1,0:T(8,128)(2,1)S(1)}, bf16[2,64,2048]{2,1,0:T(8,128)(2,1)S(1)}, u32[]{:S(2)}, u32[]{:S(2)}) collective-permute-start(bf16[2,64,2048]{2,1,0:T(8,128)(2,1)S(1)} %slice.200), channel_id=1, source_target_pairs={{0,3},{1,0},{2,1},{3,2},{4,7},{5,4},{6,5},{7,6},{8,11},{9,8},{10,9... | collective-permute-start | bytes 1572872 | tf_op jit(solution)/shard_map/ppermute | solution.py:347
  228.6 16.9 %collective-permute-start.29 = (bf16[2,64,2048]{2,1,0:T(8,128)(2,1)S(1)}, bf16[2,64,2048]{2,1,0:T(8,128)(2,1)S(1)}, u32[]{:S(2)}, u32[]{:S(2)}) collective-permute-start(bf16[2,64,2048]{2,1,0:T(8,128)(2,1)S(1)} %slice.197), channel_id=1, source_target_pairs={{0,4},{1,5},{2,6},{3,7},{4,8},{5,9},{6,10},{7,11},{8,12},{9,13},{1... | collective-permute-start | bytes 1572872 | tf_op jit(solution)/shard_map/ppermute | solution.py:347
  230.9 14.6 %collective-permute-start.30 = (bf16[2,64,2048]{2,1,0:T(8,128)(2,1)S(1)}, bf16[2,64,2048]{2,1,0:T(8,128)(2,1)S(1)}, u32[]{:S(2)}, u32[]{:S(2)}) collective-permute-start(bf16[2,64,2048]{2,1,0:T(8,128)(2,1)S(1)} %slice.198), channel_id=1, source_target_pairs={{0,12},{1,13},{2,14},{3,15},{4,0},{5,1},{6,2},{7,3},{8,4},{9,5},{1... | collective-permute-start | bytes 1572872 | tf_op jit(solution)/shard_map/ppermute | solution.py:347
  257.3 19.0 %collective-permute-start.34 = (bf16[2,64,2048]{2,1,0:T(8,128)(2,1)S(1)}, bf16[2,64,2048]{2,1,0:T(8,128)(2,1)S(1)}, u32[]{:S(2)}, u32[]{:S(2)}) collective-permute-start(bf16[2,64,2048]{2,1,0:T(8,128)(2,1)S(1)} %get-tuple-element.110), channel_id=1, source_target_pairs={{0,4},{1,5},{2,6},{3,7},{4,8},{5,9},{6,10},{7,11},{8,12},{9,13},{1... | collective-permute-start | bytes 1572872 | tf_op jit(solution)/shard_map/ppermute | solution.py:347
  257.4 19.0 %collective-permute-start.35 = (bf16[2,64,2048]{2,1,0:T(8,128)(2,1)S(1)}, bf16[2,64,2048]{2,1,0:T(8,128)(2,1)S(1)}, u32[]{:S(2)}, u32[]{:S(2)}) collective-permute-start(bf16[2,64,2048]{2,1,0:T(8,128)(2,1)S(1)} %get-tuple-element.109), channel_id=1, source_target_pairs={{0,12},{1,13},{2,14},{3,15},{4,0},{5,1},{6,2},{7,3},{8,4},{9,5},{1... | collective-permute-start | bytes 1572872 | tf_op jit(solution)/shard_map/ppermute | solution.py:347
  260.7 15.7 %collective-permute-start.36 = (bf16[2,64,2048]{2,1,0:T(8,128)(2,1)S(1)}, bf16[2,64,2048]{2,1,0:T(8,128)(2,1)S(1)}, u32[]{:S(2)}, u32[]{:S(2)}) collective-permute-start(bf16[2,64,2048]{2,1,0:T(8,128)(2,1)S(1)} %get-tuple-element.108), channel_id=1, source_target_pairs={{0,1},{1,2},{2,3},{3,0},{4,5},{5,6},{6,7},{7,4},{8,9},{9,10},{10,1... | collective-permute-start | bytes 1572872 | tf_op jit(solution)/shard_map/ppermute | solution.py:347
  261.0 15.3 %collective-permute-start.37 = (bf16[2,64,2048]{2,1,0:T(8,128)(2,1)S(1)}, bf16[2,64,2048]{2,1,0:T(8,128)(2,1)S(1)}, u32[]{:S(2)}, u32[]{:S(2)}) collective-permute-start(bf16[2,64,2048]{2,1,0:T(8,128)(2,1)S(1)} %get-tuple-element.107), channel_id=1, source_target_pairs={{0,3},{1,0},{2,1},{3,2},{4,7},{5,4},{6,5},{7,6},{8,11},{9,8},{10,9... | collective-permute-start | bytes 1572872 | tf_op jit(solution)/shard_map/ppermute | solution.py:347
  276.6 23.4 %collective-permute-start.38 = (bf16[4,64,2048]{2,1,0:T(8,128)(2,1)S(1)}, bf16[4,64,2048]{2,1,0:T(8,128)(2,1)S(1)}, u32[]{:S(2)}, u32[]{:S(2)}) collective-permute-start(bf16[4,64,2048]{2,1,0:T(8,128)(2,1)S(1)} %pad_maximum_fusion.6), channel_id=1, source_target_pairs={{0,4},{1,5},{2,6},{3,7},{4,8},{5,9},{6,10},{7,11},{8,12},{9,13},{1... | collective-permute-start | bytes 3145736 | tf_op jit(solution)/shard_map/ppermute | solution.py:347
  276.9 23.1 %collective-permute-start.39 = (bf16[4,64,2048]{2,1,0:T(8,128)(2,1)S(1)}, bf16[4,64,2048]{2,1,0:T(8,128)(2,1)S(1)}, u32[]{:S(2)}, u32[]{:S(2)}) collective-permute-start(bf16[4,64,2048]{2,1,0:T(8,128)(2,1)S(1)} %pad_maximum_fusion.7), channel_id=1, source_target_pairs={{0,12},{1,13},{2,14},{3,15},{4,0},{5,1},{6,2},{7,3},{8,4},{9,5},{1... | collective-permute-start | bytes 3145736 | tf_op jit(solution)/shard_map/ppermute | solution.py:347
  280.5 26.5 %collective-permute-start.43 = (bf16[4,64,2048]{2,1,0:T(8,128)(2,1)S(1)}, bf16[4,64,2048]{2,1,0:T(8,128)(2,1)S(1)}, u32[]{:S(2)}, u32[]{:S(2)}) collective-permute-start(bf16[4,64,2048]{2,1,0:T(8,128)(2,1)S(1)} %pad_maximum_fusion.8), channel_id=1, source_target_pairs={{0,1},{1,2},{2,3},{3,0},{4,5},{5,6},{6,7},{7,4},{8,9},{9,10},{10,1... | collective-permute-start | bytes 3145736 | tf_op jit(solution)/shard_map/ppermute | solution.py:347
  280.8 26.2 %collective-permute-start.44 = (bf16[4,64,2048]{2,1,0:T(8,128)(2,1)S(1)}, bf16[4,64,2048]{2,1,0:T(8,128)(2,1)S(1)}, u32[]{:S(2)}, u32[]{:S(2)}) collective-permute-start(bf16[4,64,2048]{2,1,0:T(8,128)(2,1)S(1)} %pad_maximum_fusion.9), channel_id=1, source_target_pairs={{0,3},{1,0},{2,1},{3,2},{4,7},{5,4},{6,5},{7,6},{8,11},{9,8},{10,9... | collective-permute-start | bytes 3145736 | tf_op jit(solution)/shard_map/ppermute | solution.py:347
  300.6 13.9 %collective-permute-start.40 = (bf16[64,2048]{1,0:T(8,128)(2,1)S(1)}, bf16[64,2048]{1,0:T(8,128)(2,1)S(1)}, u32[]{:S(2)}, u32[]{:S(2)}) collective-permute-start(bf16[64,2048]{1,0:T(8,128)(2,1)S(1)} %get-tuple-element.101), channel_id=1, source_target_pairs={{0,1},{1,2},{2,3},{3,0},{4,5},{5,6},{6,7},{7,4},{8,9},{9,10},{10,1... | collective-permute-start | bytes 786440 | tf_op jit(solution)/shard_map/ppermute | solution.py:347
  300.7 13.9 %collective-permute-start.41 = (bf16[64,2048]{1,0:T(8,128)(2,1)S(1)}, bf16[64,2048]{1,0:T(8,128)(2,1)S(1)}, u32[]{:S(2)}, u32[]{:S(2)}) collective-permute-start(bf16[64,2048]{1,0:T(8,128)(2,1)S(1)} %get-tuple-element.103), channel_id=1, source_target_pairs={{0,3},{1,0},{2,1},{3,2},{4,7},{5,4},{6,5},{7,6},{8,11},{9,8},{10,9... | collective-permute-start | bytes 786440 | tf_op jit(solution)/shard_map/ppermute | solution.py:347
  304.0 10.7 %collective-permute-start.42 = (bf16[64,2048]{1,0:T(8,128)(2,1)S(1)}, bf16[64,2048]{1,0:T(8,128)(2,1)S(1)}, u32[]{:S(2)}, u32[]{:S(2)}) collective-permute-start(bf16[64,2048]{1,0:T(8,128)(2,1)S(1)} %get-tuple-element.102), channel_id=1, source_target_pairs={{0,2},{1,3},{2,0},{3,1},{4,6},{5,7},{6,4},{7,5},{8,10},{9,11},{10,... | collective-permute-start | bytes 786440 | tf_op jit(solution)/shard_map/ppermute | solution.py:347
  307.6 10.3 %collective-permute-start.45 = (bf16[64,2048]{1,0:T(8,128)(2,1)S(1)}, bf16[64,2048]{1,0:T(8,128)(2,1)S(1)}, u32[]{:S(2)}, u32[]{:S(2)}) collective-permute-start(bf16[64,2048]{1,0:T(8,128)(2,1)S(1)} %get-tuple-element.104), channel_id=1, source_target_pairs={{0,4},{1,5},{2,6},{3,7},{4,8},{5,9},{6,10},{7,11},{8,12},{9,13},{1... | collective-permute-start | bytes 786440 | tf_op jit(solution)/shard_map/ppermute | solution.py:347
  307.7 10.2 %collective-permute-start.46 = (bf16[64,2048]{1,0:T(8,128)(2,1)S(1)}, bf16[64,2048]{1,0:T(8,128)(2,1)S(1)}, u32[]{:S(2)}, u32[]{:S(2)}) collective-permute-start(bf16[64,2048]{1,0:T(8,128)(2,1)S(1)} %get-tuple-element.106), channel_id=1, source_target_pairs={{0,12},{1,13},{2,14},{3,15},{4,0},{5,1},{6,2},{7,3},{8,4},{9,5},{1... | collective-permute-start | bytes 786440 | tf_op jit(solution)/shard_map/ppermute | solution.py:347
  314.6 7.9 %collective-permute-start.47 = (bf16[64,2048]{1,0:T(8,128)(2,1)S(1)}, bf16[64,2048]{1,0:T(8,128)(2,1)S(1)}, u32[]{:S(2)}, u32[]{:S(2)}) collective-permute-start(bf16[64,2048]{1,0:T(8,128)(2,1)S(1)} %get-tuple-element.105), channel_id=1, source_target_pairs={{0,8},{1,9},{2,10},{3,11},{4,12},{5,13},{6,14},{7,15},{8,0},{9,1},... | collective-permute-start | bytes 786440 | tf_op jit(solution)/shard_map/ppermute | solution.py:347
  (32 other events, 507.5 us)
Sparse Core Ops, SparseCore 0:
  78.3 75.8 all-gather.2
